TPU v7x, 32 devices: a whole 2x2x4 slice. The times are simulated.
32 devices in a mesh: lat: 4 (over x, core), lon: 8 (over z, y).
Axes of the slice: x: 2, y: 2, z: 4, core: 2. Of those that a mesh axis runs over, the one named last changes fastest.
Arguments:
- control: float32 [20, 4, 64, 1024], P(None, None, 'lat', 'lon'), may hold values from -6 to 6
- kappa: float32 [64, 1024], P('lat', 'lon'), may hold values from 0.05 to 0.49
- sea_mask: int32 [64, 1024], P('lat', 'lon'), may hold values 0 or 1
- vert_coef: float32 [20, 64, 1024], P(None, 'lat', 'lon'), may hold values from 0.5 to 20
- stencil_offsets: int32 [8, 1024, 1024], P(None, ('lat', 'lon')), may hold values from 0 to 2047
- stencil_weights: float32 [8, 1024, 1024], P(None, ('lat', 'lon')), may hold values from 0.05 to 0.3
- slot_target: int32 [1024, 1024], P(('lat', 'lon')), may hold values from 0 to 8191
- observed: float32 [262144], P(('lat', 'lon')), may hold values from -6 to 6
- inv_error: float32 [262144], P(('lat', 'lon')), may hold values from 0.5 to 2
Outputs:
- increment: float32 [20, 4, 64, 1024], P(None, None, 'lat', 'lon')
- misfit: float32 [262144], P(('lat', 'lon'))
Inputs may be any that keep to these rules, and one draw needn't show every extreme that they name: `stencil_offsets`: an offset indexes one horizontal cell of one device's tile, as row * 128 + column.
All inputs are finite; a program needn't handle non-finite values. No bound on the sum of `sea_mask` on one device may be relied on, other than what follows from the above.
Results may differ from a plain program's by a relative error of at most 0.00002.
Values sent between devices are 32-bit elements; how exact they have to be, the bound alone decides.
A program may use at most 64 MiB of HBM per device.

v0:
```python
import jax
import jax.numpy as jnp
from jax import lax
from jax.sharding import PartitionSpec as P

STEPS = 10


def with_halo(cells, sides, width, closed):
    for axis, dim in sides:
        count = lax.axis_size(axis)
        ends = count if closed else count - 1
        head = lax.slice_in_dim(cells, 0, width, axis=dim)
        tail = lax.slice_in_dim(cells, cells.shape[dim] - width, cells.shape[dim], axis=dim)
        cells = jnp.concatenate(
            [
                lax.ppermute(tail, axis, [(i, (i + 1) % count) for i in range(ends)]),
                cells,
                lax.ppermute(head, axis, [((i + 1) % count, i) for i in range(ends)]),
            ],
            axis=dim,
        )
    return cells


def diffuse_step(wide, gwide):
    centre = wide[:, 1:-1, 1:-1]
    flux = gwide[2:, 1:-1] * (wide[:, 2:, 1:-1] - centre)
    flux = flux + gwide[:-2, 1:-1] * (wide[:, :-2, 1:-1] - centre)
    flux = flux + gwide[1:-1, 2:] * (wide[:, 1:-1, 2:] - centre)
    flux = flux + gwide[1:-1, :-2] * (wide[:, 1:-1, :-2] - centre)
    return centre + gwide[1:-1, 1:-1] * flux


def column_solve(rhs, vert_coef):
    upper_coef = jnp.concatenate([vert_coef[1:], jnp.zeros_like(vert_coef[:1])], axis=0)
    diag = 1.0 + vert_coef + upper_coef
    lower = -vert_coef
    upper = -upper_coef

    def forward(carry, items):
        cprev, dprev = carry
        low, mid, up, right = items
        denom = mid - low * cprev
        cnew = up / denom
        dnew = (right - low[None] * dprev) / denom[None]
        return ((cnew, dnew), (cnew, dnew))

    init = (jnp.zeros(rhs.shape[2:], jnp.float32), jnp.zeros(rhs.shape[1:], jnp.float32))
    _, (cstore, dstore) = lax.scan(forward, init, (lower, diag, upper, rhs))

    def backward(ynext, items):
        cval, dval = items
        yval = dval - cval[None] * ynext
        return (yval, yval)

    _, result = lax.scan(
        backward, jnp.zeros(rhs.shape[1:], jnp.float32), (cstore, dstore), reverse=True
    )
    return result


def per_device(
    control,
    kappa,
    sea_mask,
    vert_coef,
    stencil_offsets,
    stencil_weights,
    slot_target,
    observed,
    inv_error,
):
    levels, fields, rows, cols = control.shape
    coef = kappa * sea_mask.astype(jnp.float32)
    field = control.reshape(levels * fields, rows, cols)
    depth = 1

    def one_round(turn, state):
        stacked = jnp.concatenate([state, coef[None]], axis=0)
        wide = with_halo(stacked, (("lon", 2),), depth, True)
        wide = with_halo(wide, (("lat", 1),), depth, False)
        inner = wide[:-1]
        gwide = wide[-1]
        inner = diffuse_step(inner, gwide)
        return inner

    field = lax.fori_loop(0, STEPS // depth, one_round, field)
    increment = column_solve(field.reshape(levels, fields, rows, cols), vert_coef)
    flat = increment.reshape(-1)
    slots = stencil_offsets.shape[2]
    layer = jnp.arange(slots, dtype=jnp.int32) % (levels * fields)
    full_index = stencil_offsets + (layer * (rows * cols))[None, None, :]
    gathered = flat[full_index]
    partial_value = jnp.sum(gathered * stencil_weights, axis=0)
    received = lax.all_to_all(
        partial_value, ("lat", "lon"), split_axis=0, concat_axis=0, tiled=True
    )
    totals = (
        jnp.zeros(observed.shape, jnp.float32).at[slot_target.reshape(-1)].add(received.reshape(-1))
    )
    misfit = (totals - observed) * inv_error
    return (increment, misfit)


def solution(mesh):
    return jax.shard_map(
        per_device,
        mesh=mesh,
        in_specs=(
            P(None, None, "lat", "lon"),
            P("lat", "lon"),
            P("lat", "lon"),
            P(None, "lat", "lon"),
            P(None, ("lat", "lon"), None),
            P(None, ("lat", "lon"), None),
            P(("lat", "lon"), None),
            P(("lat", "lon")),
            P(("lat", "lon")),
        ),
        out_specs=(P(None, None, "lat", "lon"), P(("lat", "lon"))),
        check_vma=False,
    )
```

profile of v0, /device:TPU:0, one launch (start us, length us, event | category | flops | bytes accessed | tf_op | source)
XLA Modules:
  0.0 1857.7 jit_solution(15570098002544610223)
XLA Ops:
  2.4 173.5 %while.44 = (s32[]{:T(128)}, f32[80,16,128]{2,1,0:T(8,128)S(1)}, f32[16,128]{1,0:T(8,128)S(1)}, s32[]{:T(128)}) while((s32[]{:T(128)}, f32[80,16,128]{2,1,0:T(8,128)S(1)}, f32[16,128]{1,0:T(8,128)S(1)}, s32[]{:T(128)}) %tuple.107), condition=%wide.region_1.0_spmd, body=%wide.region_0.0_spmd.sunk | while | flops 4173474 | bytes 5466837 | solution.py:88
  3.0 3.0 collective-permute-start
  6.4 3.1 collective-permute-start.1
  14.7 3.7 collective-permute-done.3
  21.9 3.6 collective-permute-start.1
  28.2 4.1 collective-permute-start.2
  33.6 2.2 collective-permute-done.3
  38.1 4.7 collective-permute-start.1
  45.5 4.1 collective-permute-start.2
  50.9 2.2 collective-permute-done.3
  55.5 4.7 collective-permute-start.1
  62.9 4.1 collective-permute-start.2
  68.3 2.2 collective-permute-done.3
  72.8 4.7 collective-permute-start.1
  80.2 4.1 collective-permute-start.2
  85.6 2.2 collective-permute-done.3
  90.2 4.7 collective-permute-start.1
  97.6 4.1 collective-permute-start.2
  103.0 2.2 collective-permute-done.3
  107.5 4.7 collective-permute-start.1
  114.9 4.1 collective-permute-start.2
  120.3 2.2 collective-permute-done.3
  124.9 4.7 collective-permute-start.1
  132.3 4.1 collective-permute-start.2
  137.7 2.2 collective-permute-done.3
  142.2 4.7 collective-permute-start.1
  149.6 4.1 collective-permute-start.2
  155.0 2.2 collective-permute-done.3
  159.6 4.7 collective-permute-start.1
  167.0 4.1 collective-permute-start.2
  172.4 2.2 collective-permute-done.3
  176.0 27.4 %while.45 = (s32[]{:T(128)}, f32[16,128]{1,0:T(8,128)S(1)}, f32[4,16,128]{2,1,0:T(8,128)S(1)}, f32[20,16,128]{2,1,0:T(8,128)}, f32[20,4,16,128]{3,2,1,0:T(8,128)...) while((s32[]{:T(128)}, f32[16,128]{1,0:T(8,128)S(1)}, ...), condition=%wide.region_3.4_spmd.clone, body=%wide.region_2.3_spmd.clone.sunk | while | flops 40963 | bytes 213628 | solution.py:50
  176.0 1.4 bitcast_dynamic-update-slice_fusion.6
  178.9 1.3 bitcast_dynamic-update-slice_fusion.6
  180.2 1.3 bitcast_dynamic-update-slice_fusion.6
  181.6 1.3 bitcast_dynamic-update-slice_fusion.6
  185.7 1.3 bitcast_dynamic-update-slice_fusion.6
  187.1 1.3 bitcast_dynamic-update-slice_fusion.6
  188.4 1.3 bitcast_dynamic-update-slice_fusion.6
  192.5 1.3 bitcast_dynamic-update-slice_fusion.6
  193.9 1.3 bitcast_dynamic-update-slice_fusion.6
  195.3 1.3 bitcast_dynamic-update-slice_fusion.6
  203.5 14.7 while.46
  219.1 1449.2 %gather_fusion = f32[262144]{0:T(1024)S(1)} fusion(f32[163840]{0:T(1024)S(1)} %bitcast.53, s32[262144]{0:T(1024)S(1)} %broadcast_clamp_fusion), kind=kCustom, calls=%fused_computation | custom fusion | bytes 3145728 | tf_op jit(solution)/shard_map/gather | solution.py:94
  1668.5 1.4 multiply_reduce_fusion
  1670.6 7.7 all-to-all-start
  1678.6 7.4 all-to-all-done
  1686.0 171.1 %scatter_custom_fusion = f32[8192]{0:T(1024)S(1)} fusion(s32[32768]{0:T(1024)S(1)} %bitcast.65, f32[32768]{0:T(1024)S(1)} %bitcast.64, f32[]{:T(128)} %constant.80.clone.1), kind=kCustom, calls=%fused_computation.59 | custom fusion | flops 32768 | bytes 32772 | tf_op jit(solution)/shard_map/scatter-add | solution.py:100
  (257 shorter events, 97.2 us)
Async XLA Ops:
  0.6 0.9 copy-start.3
  0.6 1.0 slice-start
  0.6 1.8 copy-start.1
  3.0 7.7 collective-permute-start
  6.4 4.7 collective-permute-start.1
  12.1 2.6 collective-permute-start.2
  13.4 5.1 collective-permute-start.3
  20.4 6.4 collective-permute-start
  21.9 5.3 collective-permute-start.1
  28.2 5.4 collective-permute-start.2
  32.3 3.6 collective-permute-start.3
  37.8 6.4 collective-permute-start
  38.1 6.4 collective-permute-start.1
  45.5 5.4 collective-permute-start.2
  49.6 3.6 collective-permute-start.3
  55.1 6.4 collective-permute-start
  55.5 6.4 collective-permute-start.1
  62.9 5.4 collective-permute-start.2
  67.0 3.6 collective-permute-start.3
  72.5 6.4 collective-permute-start
  72.8 6.4 collective-permute-start.1
  80.2 5.4 collective-permute-start.2
  84.3 3.6 collective-permute-start.3
  89.8 6.4 collective-permute-start
  90.2 6.4 collective-permute-start.1
  97.6 5.4 collective-permute-start.2
  101.7 3.6 collective-permute-start.3
  107.2 6.4 collective-permute-start
  107.5 6.4 collective-permute-start.1
  114.9 5.4 collective-permute-start.2
  119.0 3.6 collective-permute-start.3
  124.5 6.4 collective-permute-start
  124.9 6.4 collective-permute-start.1
  132.3 5.4 collective-permute-start.2
  136.4 3.6 collective-permute-start.3
  141.9 6.4 collective-permute-start
  142.2 6.4 collective-permute-start.1
  149.6 5.4 collective-permute-start.2
  153.7 3.6 collective-permute-start.3
  159.2 6.4 collective-permute-start
  159.6 6.4 collective-permute-start.1
  167.0 5.4 collective-permute-start.2
  171.1 3.6 collective-permute-start.3
  176.0 42.2 %copy-start.2 = (s32[8,32,1024]{2,1,0:T(8,128)S(1)}, s32[8,32,1024]{2,1,0:T(8,128)}, u32[]{:S(2)}) copy-start(s32[8,32,1024]{2,1,0:T(8,128)} %param.19) | copy-start | bytes 3145732
  1670.6 7.7 copy-start.4
  1670.6 15.5 all-to-all-start
  1678.4 178.7 %copy-start.6 = (f32[8192]{0:T(1024)S(1)}, f32[8192]{0:T(1024)}, u32[]{:S(2)}) copy-start(f32[8192]{0:T(1024)} %param.22) | copy-start | bytes 98308
  1678.6 178.5 %copy-start.5 = (f32[8192]{0:T(1024)S(1)}, f32[8192]{0:T(1024)}, u32[]{:S(2)}) copy-start(f32[8192]{0:T(1024)} %param.23) | copy-start | bytes 98308
  (3 other events, 2.4 us)
where the time goes:
time: 1860 us
  local copies, waits for them, and re-layouts  1480 us (80%)
  other arithmetic  222 us (12%)
  starting transfers between devices  107 us (6%)
  waiting for transfers between devices  44.2 us (2%)
    gather x2, local copies, waits for them, and re-layouts, per_device(): gathered = flat[full_index]  1450 us
    scatter-add x1, other arithmetic, per_device(): jnp.zeros(observed.shape, jnp.float32).at[slot_target.reshape(-1)]  171 us
    ppermute x20, starting transfers between devices, with_halo(): lax.ppermute(head, axis, [((i + 1) % count, i) for i in range(ends)])  57.3 us
    ppermute x20, starting transfers between devices, with_halo(): lax.ppermute(tail, axis, [(i, (i + 1) % count) for i in range(ends)])  42.2 us
  transfers between devices with their start and end apart: 41, of which 21 were waited for; matrix products, arithmetic and copies ran while one was open for 0% of the time, Pallas kernels for 0%

commit v1 on v0

--- a/solution.py
+++ b/solution.py
@@ -1,9 +1,15 @@
+import functools
+
 import jax
 import jax.numpy as jnp
 from jax import lax
+from jax.experimental import pallas as pl
+from jax.experimental.pallas import tpu as pltpu
 from jax.sharding import PartitionSpec as P
 
 STEPS = 10
+LANES = 128
+SUB = 8
 
 
 def with_halo(cells, sides, width, closed):
@@ -60,6 +66,125 @@
     return result
 
 
+def pick(table, row, col):
+    level = [jnp.take_along_axis(t, col, axis=1) for t in table]
+    bit = 1
+    while len(level) > 1:
+        odd = (row & bit) != 0
+        level = [jnp.where(odd, level[i + 1], level[i]) for i in range(0, len(level), 2)]
+        bit *= 2
+    return level[0]
+
+
+def gather_kernel(rows, layers, owners, inc_ref, off_ref, w_ref, out_ref, off_t, w_t, acc):
+    cap = off_ref.shape[1]
+    groups = off_ref.shape[0] // LANES
+    turns = -(-cap // layers)
+    padded = turns * layers
+    if padded > cap:
+        for g in range(groups):
+            off_t[g, cap:padded, :] = jnp.zeros((padded - cap, LANES), jnp.int32)
+            w_t[g, cap:padded, :] = jnp.zeros((padded - cap, LANES), jnp.float32)
+    for g in range(groups):
+        for c in range(cap // LANES):
+            here = pl.ds(c * LANES, LANES)
+            off_t[g, here, :] = off_ref[pl.ds(g * LANES, LANES), here].T
+            w_t[g, here, :] = w_ref[pl.ds(g * LANES, LANES), here].T
+
+    def one_group(lg, carry):
+        base = pl.multiple_of(lg * SUB, SUB)
+        table = [inc_ref[pl.ds(base * rows + r, SUB, stride=rows), :] for r in range(rows)]
+        for m in range(turns):
+            at = pl.ds(m * layers + base, SUB)
+            total = None
+            for g in range(groups):
+                idx = off_t[g, at, :]
+                term = pick(table, idx >> 7, idx & (LANES - 1)) * w_t[g, at, :]
+                total = term if total is None else total + term
+            acc[at, :] = total
+        return carry
+
+    lax.fori_loop(0, layers // SUB, one_group, 0)
+    for c in range(cap // LANES):
+        here = pl.ds(c * LANES, LANES)
+        block = acc[here, :].T
+        total = block[:owners]
+        for k in range(1, LANES // owners):
+            total = total + block[k * owners : (k + 1) * owners]
+        out_ref[:, here] = total
+
+
+def gather_partials(increment, offsets, weights):
+    layers, rows, cols = increment.shape
+    sten, owners, cap = offsets.shape
+    groups = sten * owners // LANES
+    padded = -(-cap // layers) * layers
+    return pl.pallas_call(
+        functools.partial(gather_kernel, rows, layers, owners),
+        out_shape=jax.ShapeDtypeStruct((owners, cap), jnp.float32),
+        in_specs=[pl.BlockSpec(memory_space=pltpu.VMEM)] * 3,
+        out_specs=pl.BlockSpec(memory_space=pltpu.VMEM),
+        scratch_shapes=[
+            pltpu.VMEM((groups, padded, LANES), jnp.int32),
+            pltpu.VMEM((groups, padded, LANES), jnp.float32),
+            pltpu.VMEM((padded, LANES), jnp.float32),
+        ],
+        compiler_params=pltpu.CompilerParams(vmem_limit_bytes=32 * 1024 * 1024),
+        name="gather_partials",
+    )(
+        increment.reshape(layers * rows, cols),
+        offsets.reshape(sten * owners, cap),
+        weights.reshape(sten * owners, cap),
+    )
+
+
+def split_parts(v):
+    first = v.astype(jnp.bfloat16).astype(jnp.float32)
+    rest = v - first
+    second = rest.astype(jnp.bfloat16).astype(jnp.float32)
+    return first, second, rest - second
+
+
+def spread(v, t, high):
+    cap = v.shape[1]
+    hit = lax.broadcasted_iota(jnp.int32, (high, cap), 0) == (t >> 7)
+    ones = lax.broadcasted_iota(jnp.int32, (LANES, cap), 0) == (t & (LANES - 1))
+    left = jnp.concatenate(
+        [jnp.where(hit, part, 0.0).astype(jnp.bfloat16) for part in split_parts(v)], axis=0
+    )
+    right = jnp.where(ones, 1.0, 0.0).astype(jnp.bfloat16)
+    return lax.dot_general(
+        left, right, (((1,), (1,)), ((), ())), preferred_element_type=jnp.float32
+    )
+
+
+def scatter_kernel(rec_ref, tgt_ref, obs_ref, err_ref, out_ref, acc):
+    high = obs_ref.shape[0]
+    acc[...] = jnp.zeros_like(acc)
+
+    def one_source(p, carry):
+        acc[...] += spread(rec_ref[pl.ds(p, 1), :], tgt_ref[pl.ds(p, 1), :], high)
+        return carry
+
+    lax.fori_loop(0, rec_ref.shape[0], one_source, 0)
+    total = acc[:high] + acc[high : 2 * high] + acc[2 * high :]
+    out_ref[...] = (total - obs_ref[...]) * err_ref[...]
+
+
+def scatter_misfit(received, target, observed, inv_error):
+    high = observed.shape[0] // LANES
+    out = pl.pallas_call(
+        scatter_kernel,
+        out_shape=jax.ShapeDtypeStruct((high, LANES), jnp.float32),
+        in_specs=[pl.BlockSpec(memory_space=pltpu.VMEM)] * 4,
+        out_specs=pl.BlockSpec(memory_space=pltpu.VMEM),
+        scratch_shapes=[pltpu.VMEM((3 * high, LANES), jnp.float32)],
+        compiler_params=pltpu.CompilerParams(vmem_limit_bytes=32 * 1024 * 1024),
+        name="scatter_misfit",
+    )(received, target, observed.reshape(high, LANES), inv_error.reshape(high, LANES))
+    return out.reshape(-1)
+
+
 def per_device(
     control,
     kappa,
@@ -87,19 +212,13 @@
 
     field = lax.fori_loop(0, STEPS // depth, one_round, field)
     increment = column_solve(field.reshape(levels, fields, rows, cols), vert_coef)
-    flat = increment.reshape(-1)
-    slots = stencil_offsets.shape[2]
-    layer = jnp.arange(slots, dtype=jnp.int32) % (levels * fields)
-    full_index = stencil_offsets + (layer * (rows * cols))[None, None, :]
-    gathered = flat[full_index]
-    partial_value = jnp.sum(gathered * stencil_weights, axis=0)
+    partial_value = gather_partials(
+        increment.reshape(levels * fields, rows, cols), stencil_offsets, stencil_weights
+    )
     received = lax.all_to_all(
         partial_value, ("lat", "lon"), split_axis=0, concat_axis=0, tiled=True
     )
-    totals = (
-        jnp.zeros(observed.shape, jnp.float32).at[slot_target.reshape(-1)].add(received.reshape(-1))
-    )
-    misfit = (totals - observed) * inv_error
+    misfit = scatter_misfit(received, slot_target, observed, inv_error)
     return (increment, misfit)
 
 

time: 1860 us -> 291 us (0.16)
  local copies, waits for them, and re-layouts: 1480 us -> 44.4 us
  other arithmetic: 222 us -> 72 us
    gather x2 -> x0, local copies, waits for them, and re-layouts: 1450 us -> none  [per_device(): gathered = flat[full_index]]
    scatter-add x1 -> x0, other arithmetic: 171 us -> none  [per_device(): jnp.zeros(observed.shape, jnp.float32).at[slot_target.reshape(-1)]]
  transfers between devices with their start and end apart: 41 -> 40, of which waited for: 21 -> 20; matrix products, arithmetic and copies ran while one was open for 0% -> 3% of each run, Pallas kernels for 0% -> 0%
where the time goes in v1:
time: 291 us; the launch traced here: 287 us
  starting transfers between devices  99.6 us (34%)
  other arithmetic  72 us (25%)
  local copies, waits for them, and re-layouts  44.4 us (15%)
  waiting for transfers between devices  36.8 us (13%)
  Pallas kernels  16.4 us (6%)
  blocking collectives  15.3 us (5%)
    ppermute x20, starting transfers between devices, with_halo(): lax.ppermute(head, axis, [((i + 1) % count, i) for i in range(ends)])  57.3 us
    dynamic_update_slice x60, other arithmetic, column_solve(): _, (cstore, dstore) = lax.scan(forward, init, (lower, diag, upper, rhs))  42.6 us
    ppermute x20, starting transfers between devices, with_halo(): lax.ppermute(tail, axis, [(i, (i + 1) % count) for i in range(ends)])  42.2 us
    ppermute x20, waiting for transfers between devices, with_halo(): lax.ppermute(head, axis, [((i + 1) % count, i) for i in range(ends)])  23.9 us
    add x10, other arithmetic, diffuse_step(): return centre + gwide[1:-1, 1:-1] * flux  19.5 us
    all_to_all x1, blocking collectives, per_device(): lax.all_to_all(partial_value, ('lat', 'lon'), split_axis=0, concat_axis=0...  15.3 us
    mul x20, local copies, waits for them, and re-layouts, backward(): yval = dval - cval[None] * ynext  14.1 us
    ppermute x20, waiting for transfers between devices, with_halo(): lax.ppermute(tail, axis, [(i, (i + 1) % count) for i in range(ends)])  12.9 us
  transfers between devices with their start and end apart: 40, of which 20 were waited for; matrix products, arithmetic and copies ran while one was open for 3% of the time, Pallas kernels for 0%

profile of v1, /device:TPU:0, one launch (start us, length us, event | category | flops | bytes accessed | tf_op | source)
XLA Modules:
  0.0 286.6 jit_solution(12382992700847122152)
XLA Ops:
  0.6 2.0 copy.69
  4.5 191.7 %while.44 = (s32[]{:T(128)}, f32[80,16,128]{2,1,0:T(8,128)}, f32[16,128]{1,0:T(8,128)S(1)}, s32[]{:T(128)}) while((s32[]{:T(128)}, f32[80,16,128]{2,1,0:T(8,128)}, f32[16,128]{1,0:T(8,128)S(1)}, s32[]{:T(128)}) %tuple.97), condition=%wide.region_1.0_spmd, body=%wide.region_0.0_spmd.sunk | while | flops 4173474 | bytes 5466837 | solution.py:213
  6.2 3.0 %collective-permute-start = (f32[81,16,1]{0,1,2:T(8,128)S(1)}, f32[81,16,1]{0,1,2:T(8,128)S(1)}, u32[]{:S(2)}, u32[]{:S(2)}) collective-permute-start(f32[81,16,1]{0,1,2:T(8,128)S(1)} %copy.30), channel_id=1, source_target_pairs={{0,1},{1,2},{2,3},{3,4},{4,5},{5,6},{6,7},{7,0},{8,9},{9,10},{10,1... | collective-permute-start | bytes 15560 | tf_op jit(solution)/shard_map/while/body/eval_jaxpr/ppermute | solution.py:23
  9.5 3.1 %collective-permute-start.1 = (f32[81,16,1]{0,1,2:T(8,128)S(1)}, f32[81,16,1]{0,1,2:T(8,128)S(1)}, u32[]{:S(2)}, u32[]{:S(2)}) collective-permute-start(f32[81,16,1]{0,1,2:T(8,128)S(1)} %copy.32), channel_id=1, source_target_pairs={{1,0},{2,1},{3,2},{4,3},{5,4},{6,5},{7,6},{0,7},{9,8},{10,9},{11,1... | collective-permute-start | bytes 15560 | tf_op jit(solution)/shard_map/while/body/eval_jaxpr/ppermute | solution.py:25
  17.9 3.7 %collective-permute-done.3 = f32[81,1,130]{2,1,0:T(1,128)S(1)} collective-permute-done((f32[81,1,130]{2,1,0:T(1,128)S(1)}, f32[81,1,130]{2,1,0:T(1,128)S(1)}, u32[]{:S(2)}, u32[]{:S(2)}) %collective-permute-start.3) | collective-permute-done | bytes 42152 | tf_op jit(solution)/shard_map/while/body/eval_jaxpr/ppermute | solution.py:25
  21.8 2.0 fusion.23
  26.9 3.6 %collective-permute-start.1 = (f32[81,16,1]{0,1,2:T(8,128)S(1)}, f32[81,16,1]{0,1,2:T(8,128)S(1)}, u32[]{:S(2)}, u32[]{:S(2)}) collective-permute-start(f32[81,16,1]{0,1,2:T(8,128)S(1)} %copy.32), channel_id=1, source_target_pairs={{1,0},{2,1},{3,2},{4,3},{5,4},{6,5},{7,6},{0,7},{9,8},{10,9},{11,1... | collective-permute-start | bytes 15560 | tf_op jit(solution)/shard_map/while/body/eval_jaxpr/ppermute | solution.py:25
  33.2 4.1 %collective-permute-start.2 = (f32[81,1,130]{2,1,0:T(1,128)S(1)}, f32[81,1,130]{2,1,0:T(1,128)S(1)}, u32[]{:S(2)}, u32[]{:S(2)}) collective-permute-start(f32[81,1,130]{2,1,0:T(1,128)S(1)} %get-tuple-element.386), channel_id=1, source_target_pairs={{0,8},{8,16},{16,24},{1,9},{9,17},{17,25},{2,10},{10,18},{18,26},{... | collective-permute-start | bytes 126368 | tf_op jit(solution)/shard_map/while/body/eval_jaxpr/ppermute | solution.py:23
  38.5 2.2 collective-permute-done.3
  40.9 2.0 fusion.23
  44.9 4.7 %collective-permute-start.1 = (f32[81,16,1]{0,1,2:T(8,128)S(1)}, f32[81,16,1]{0,1,2:T(8,128)S(1)}, u32[]{:S(2)}, u32[]{:S(2)}) collective-permute-start(f32[81,16,1]{0,1,2:T(8,128)S(1)} %copy.32), channel_id=1, source_target_pairs={{1,0},{2,1},{3,2},{4,3},{5,4},{6,5},{7,6},{0,7},{9,8},{10,9},{11,1... | collective-permute-start | bytes 15560 | tf_op jit(solution)/shard_map/while/body/eval_jaxpr/ppermute | solution.py:25
  52.3 4.1 %collective-permute-start.2 = (f32[81,1,130]{2,1,0:T(1,128)S(1)}, f32[81,1,130]{2,1,0:T(1,128)S(1)}, u32[]{:S(2)}, u32[]{:S(2)}) collective-permute-start(f32[81,1,130]{2,1,0:T(1,128)S(1)} %get-tuple-element.386), channel_id=1, source_target_pairs={{0,8},{8,16},{16,24},{1,9},{9,17},{17,25},{2,10},{10,18},{18,26},{... | collective-permute-start | bytes 126368 | tf_op jit(solution)/shard_map/while/body/eval_jaxpr/ppermute | solution.py:23
  57.7 2.2 collective-permute-done.3
  60.1 2.0 fusion.23
  64.1 4.7 %collective-permute-start.1 = (f32[81,16,1]{0,1,2:T(8,128)S(1)}, f32[81,16,1]{0,1,2:T(8,128)S(1)}, u32[]{:S(2)}, u32[]{:S(2)}) collective-permute-start(f32[81,16,1]{0,1,2:T(8,128)S(1)} %copy.32), channel_id=1, source_target_pairs={{1,0},{2,1},{3,2},{4,3},{5,4},{6,5},{7,6},{0,7},{9,8},{10,9},{11,1... | collective-permute-start | bytes 15560 | tf_op jit(solution)/shard_map/while/body/eval_jaxpr/ppermute | solution.py:25
  71.5 4.1 %collective-permute-start.2 = (f32[81,1,130]{2,1,0:T(1,128)S(1)}, f32[81,1,130]{2,1,0:T(1,128)S(1)}, u32[]{:S(2)}, u32[]{:S(2)}) collective-permute-start(f32[81,1,130]{2,1,0:T(1,128)S(1)} %get-tuple-element.386), channel_id=1, source_target_pairs={{0,8},{8,16},{16,24},{1,9},{9,17},{17,25},{2,10},{10,18},{18,26},{... | collective-permute-start | bytes 126368 | tf_op jit(solution)/shard_map/while/body/eval_jaxpr/ppermute | solution.py:23
  76.9 2.2 collective-permute-done.3
  79.3 2.0 fusion.23
  83.2 4.7 %collective-permute-start.1 = (f32[81,16,1]{0,1,2:T(8,128)S(1)}, f32[81,16,1]{0,1,2:T(8,128)S(1)}, u32[]{:S(2)}, u32[]{:S(2)}) collective-permute-start(f32[81,16,1]{0,1,2:T(8,128)S(1)} %copy.32), channel_id=1, source_target_pairs={{1,0},{2,1},{3,2},{4,3},{5,4},{6,5},{7,6},{0,7},{9,8},{10,9},{11,1... | collective-permute-start | bytes 15560 | tf_op jit(solution)/shard_map/while/body/eval_jaxpr/ppermute | solution.py:25
  90.6 4.1 %collective-permute-start.2 = (f32[81,1,130]{2,1,0:T(1,128)S(1)}, f32[81,1,130]{2,1,0:T(1,128)S(1)}, u32[]{:S(2)}, u32[]{:S(2)}) collective-permute-start(f32[81,1,130]{2,1,0:T(1,128)S(1)} %get-tuple-element.386), channel_id=1, source_target_pairs={{0,8},{8,16},{16,24},{1,9},{9,17},{17,25},{2,10},{10,18},{18,26},{... | collective-permute-start | bytes 126368 | tf_op jit(solution)/shard_map/while/body/eval_jaxpr/ppermute | solution.py:23
  96.0 2.2 collective-permute-done.3
  98.4 2.0 fusion.23
  102.4 4.7 %collective-permute-start.1 = (f32[81,16,1]{0,1,2:T(8,128)S(1)}, f32[81,16,1]{0,1,2:T(8,128)S(1)}, u32[]{:S(2)}, u32[]{:S(2)}) collective-permute-start(f32[81,16,1]{0,1,2:T(8,128)S(1)} %copy.32), channel_id=1, source_target_pairs={{1,0},{2,1},{3,2},{4,3},{5,4},{6,5},{7,6},{0,7},{9,8},{10,9},{11,1... | collective-permute-start | bytes 15560 | tf_op jit(solution)/shard_map/while/body/eval_jaxpr/ppermute | solution.py:25
  109.8 4.1 %collective-permute-start.2 = (f32[81,1,130]{2,1,0:T(1,128)S(1)}, f32[81,1,130]{2,1,0:T(1,128)S(1)}, u32[]{:S(2)}, u32[]{:S(2)}) collective-permute-start(f32[81,1,130]{2,1,0:T(1,128)S(1)} %get-tuple-element.386), channel_id=1, source_target_pairs={{0,8},{8,16},{16,24},{1,9},{9,17},{17,25},{2,10},{10,18},{18,26},{... | collective-permute-start | bytes 126368 | tf_op jit(solution)/shard_map/while/body/eval_jaxpr/ppermute | solution.py:23
  115.2 2.2 collective-permute-done.3
  117.6 2.0 fusion.23
  121.5 4.7 %collective-permute-start.1 = (f32[81,16,1]{0,1,2:T(8,128)S(1)}, f32[81,16,1]{0,1,2:T(8,128)S(1)}, u32[]{:S(2)}, u32[]{:S(2)}) collective-permute-start(f32[81,16,1]{0,1,2:T(8,128)S(1)} %copy.32), channel_id=1, source_target_pairs={{1,0},{2,1},{3,2},{4,3},{5,4},{6,5},{7,6},{0,7},{9,8},{10,9},{11,1... | collective-permute-start | bytes 15560 | tf_op jit(solution)/shard_map/while/body/eval_jaxpr/ppermute | solution.py:25
  129.0 4.1 %collective-permute-start.2 = (f32[81,1,130]{2,1,0:T(1,128)S(1)}, f32[81,1,130]{2,1,0:T(1,128)S(1)}, u32[]{:S(2)}, u32[]{:S(2)}) collective-permute-start(f32[81,1,130]{2,1,0:T(1,128)S(1)} %get-tuple-element.386), channel_id=1, source_target_pairs={{0,8},{8,16},{16,24},{1,9},{9,17},{17,25},{2,10},{10,18},{18,26},{... | collective-permute-start | bytes 126368 | tf_op jit(solution)/shard_map/while/body/eval_jaxpr/ppermute | solution.py:23
  134.3 2.2 collective-permute-done.3
  136.7 2.0 fusion.23
  140.7 4.7 %collective-permute-start.1 = (f32[81,16,1]{0,1,2:T(8,128)S(1)}, f32[81,16,1]{0,1,2:T(8,128)S(1)}, u32[]{:S(2)}, u32[]{:S(2)}) collective-permute-start(f32[81,16,1]{0,1,2:T(8,128)S(1)} %copy.32), channel_id=1, source_target_pairs={{1,0},{2,1},{3,2},{4,3},{5,4},{6,5},{7,6},{0,7},{9,8},{10,9},{11,1... | collective-permute-start | bytes 15560 | tf_op jit(solution)/shard_map/while/body/eval_jaxpr/ppermute | solution.py:25
  148.1 4.1 %collective-permute-start.2 = (f32[81,1,130]{2,1,0:T(1,128)S(1)}, f32[81,1,130]{2,1,0:T(1,128)S(1)}, u32[]{:S(2)}, u32[]{:S(2)}) collective-permute-start(f32[81,1,130]{2,1,0:T(1,128)S(1)} %get-tuple-element.386), channel_id=1, source_target_pairs={{0,8},{8,16},{16,24},{1,9},{9,17},{17,25},{2,10},{10,18},{18,26},{... | collective-permute-start | bytes 126368 | tf_op jit(solution)/shard_map/while/body/eval_jaxpr/ppermute | solution.py:23
  153.5 2.2 collective-permute-done.3
  155.9 2.0 fusion.23
  159.9 4.7 %collective-permute-start.1 = (f32[81,16,1]{0,1,2:T(8,128)S(1)}, f32[81,16,1]{0,1,2:T(8,128)S(1)}, u32[]{:S(2)}, u32[]{:S(2)}) collective-permute-start(f32[81,16,1]{0,1,2:T(8,128)S(1)} %copy.32), channel_id=1, source_target_pairs={{1,0},{2,1},{3,2},{4,3},{5,4},{6,5},{7,6},{0,7},{9,8},{10,9},{11,1... | collective-permute-start | bytes 15560 | tf_op jit(solution)/shard_map/while/body/eval_jaxpr/ppermute | solution.py:25
  167.3 4.1 %collective-permute-start.2 = (f32[81,1,130]{2,1,0:T(1,128)S(1)}, f32[81,1,130]{2,1,0:T(1,128)S(1)}, u32[]{:S(2)}, u32[]{:S(2)}) collective-permute-start(f32[81,1,130]{2,1,0:T(1,128)S(1)} %get-tuple-element.386), channel_id=1, source_target_pairs={{0,8},{8,16},{16,24},{1,9},{9,17},{17,25},{2,10},{10,18},{18,26},{... | collective-permute-start | bytes 126368 | tf_op jit(solution)/shard_map/while/body/eval_jaxpr/ppermute | solution.py:23
  172.7 2.2 collective-permute-done.3
  175.1 2.0 fusion.23
  179.0 4.7 %collective-permute-start.1 = (f32[81,16,1]{0,1,2:T(8,128)S(1)}, f32[81,16,1]{0,1,2:T(8,128)S(1)}, u32[]{:S(2)}, u32[]{:S(2)}) collective-permute-start(f32[81,16,1]{0,1,2:T(8,128)S(1)} %copy.32), channel_id=1, source_target_pairs={{1,0},{2,1},{3,2},{4,3},{5,4},{6,5},{7,6},{0,7},{9,8},{10,9},{11,1... | collective-permute-start | bytes 15560 | tf_op jit(solution)/shard_map/while/body/eval_jaxpr/ppermute | solution.py:25
  186.4 4.1 %collective-permute-start.2 = (f32[81,1,130]{2,1,0:T(1,128)S(1)}, f32[81,1,130]{2,1,0:T(1,128)S(1)}, u32[]{:S(2)}, u32[]{:S(2)}) collective-permute-start(f32[81,1,130]{2,1,0:T(1,128)S(1)} %get-tuple-element.386), channel_id=1, source_target_pairs={{0,8},{8,16},{16,24},{1,9},{9,17},{17,25},{2,10},{10,18},{18,26},{... | collective-permute-start | bytes 126368 | tf_op jit(solution)/shard_map/while/body/eval_jaxpr/ppermute | solution.py:23
  191.8 2.2 collective-permute-done.3
  194.2 2.0 fusion.23
  196.3 42.8 %while.45 = (s32[]{:T(128)}, f32[16,128]{1,0:T(8,128)S(1)}, f32[4,16,128]{2,1,0:T(8,128)S(1)}, f32[20,16,128]{2,1,0:T(8,128)}, f32[20,4,16,128]{3,2,1,0:T(8,128)...) while((s32[]{:T(128)}, f32[16,128]{1,0:T(8,128)S(1)}, ...), condition=%wide.region_3.4_spmd.clone, body=%wide.region_2.3_spmd.clone.sunk | while | flops 40963 | bytes 213628 | solution.py:56
  196.3 1.4 bitcast_dynamic-update-slice_fusion.6
  239.1 14.7 %while.46 = (s32[]{:T(128)}, f32[4,16,128]{2,1,0:T(8,128)S(1)}, f32[20,4,16,128]{3,2,1,0:T(8,128)S(1)}, f32[20,4,16,128]{3,2,1,0:T(8,128)S(1)}, f32[20,16,128]{2...) while((s32[]{:T(128)}, f32[4,16,128]{2,1,0:T(8,128)S(1)}, f32[20,4,16,128]{3,2,1,0:T(8,128)S(1)}, ...), condition=%wide.region_5.6_spmd.clone, body=%wide.region_4.5_spmd.clone.sunk | while | flops 24580 | bytes 155763 | solution.py:63
  253.8 6.8 %gather_partials.1 = f32[32,1024]{1,0:T(8,128)S(1)} custom-call(f32[1280,128]{1,0:T(8,128)S(1)} %bitcast.64, s32[256,1024]{1,0:T(8,128)S(1)} %bitcast.54, f32[256,1024]{1,0:T(8,128)S(1)} %bitcast.55), custom_call_target="tpu_custom_call" | custom-call | tf_op jit(solution)/shard_map/gather_partials/pallas_call | solution.py:122
  260.8 15.3 %all_to_all.11 = f32[32,1,1024]{2,1,0:T(1,128)S(1)} all-to-all(f32[32,1,1024]{2,1,0:T(1,128)S(1)} %copy.22), channel_id=1, replica_groups=mesh['lat'=4,'lon'=8] {'lat','lon'}, dimensions={0} | all-to-all | bytes 262144 | tf_op jit(solution)/shard_map/all_to_all | solution.py:218
  276.9 9.7 %scatter_misfit.1 = f32[64,128]{1,0:T(8,128)} custom-call(f32[32,1024]{1,0:T(8,128)S(1)} %bitcast.57, s32[32,1024]{1,0:T(8,128)S(1)} %copy-done.2, f32[64,128]{1,0:T(8,128)S(1)} %bitcast.58, f32[64,128]{1,0:T(8,128)S(1)} %bitcast.59), custom_call_target="tpu_custom_call" | custom-call | tf_op jit(solution)/shard_map/scatter_misfit/pallas_call | solution.py:176
  (249 shorter events, 122.0 us)
Async XLA Ops:
  2.6 0.9 copy-start.6
  2.6 1.0 slice-start
  4.4 249.4 %copy-start.1 = (f32[8,32,1024]{2,1,0:T(8,128)S(1)}, f32[8,32,1024]{2,1,0:T(8,128)}, u32[]{:S(2)}) copy-start(f32[8,32,1024]{2,1,0:T(8,128)} %param.20) | copy-start | bytes 3145732
  6.2 7.7 %collective-permute-start = (f32[81,16,1]{0,1,2:T(8,128)S(1)}, f32[81,16,1]{0,1,2:T(8,128)S(1)}, u32[]{:S(2)}, u32[]{:S(2)}) collective-permute-start(f32[81,16,1]{0,1,2:T(8,128)S(1)} %copy.30), channel_id=1, source_target_pairs={{0,1},{1,2},{2,3},{3,4},{4,5},{5,6},{6,7},{7,0},{8,9},{9,10},{10,1... | collective-permute-start | bytes 15560 | tf_op jit(solution)/shard_map/while/body/eval_jaxpr/ppermute | solution.py:23
  9.5 4.7 %collective-permute-start.1 = (f32[81,16,1]{0,1,2:T(8,128)S(1)}, f32[81,16,1]{0,1,2:T(8,128)S(1)}, u32[]{:S(2)}, u32[]{:S(2)}) collective-permute-start(f32[81,16,1]{0,1,2:T(8,128)S(1)} %copy.32), channel_id=1, source_target_pairs={{1,0},{2,1},{3,2},{4,3},{5,4},{6,5},{7,6},{0,7},{9,8},{10,9},{11,1... | collective-permute-start | bytes 15560 | tf_op jit(solution)/shard_map/while/body/eval_jaxpr/ppermute | solution.py:25
  15.3 2.6 collective-permute-start.2
  16.6 5.1 %collective-permute-start.3 = (f32[81,1,130]{2,1,0:T(1,128)S(1)}, f32[81,1,130]{2,1,0:T(1,128)S(1)}, u32[]{:S(2)}, u32[]{:S(2)}) collective-permute-start(f32[81,1,130]{2,1,0:T(1,128)S(1)} %get-tuple-element.387), channel_id=1, source_target_pairs={{8,0},{16,8},{24,16},{9,1},{17,9},{25,17},{10,2},{18,10},{26,18},{... | collective-permute-start | bytes 126368 | tf_op jit(solution)/shard_map/while/body/eval_jaxpr/ppermute | solution.py:25
  25.4 6.4 %collective-permute-start = (f32[81,16,1]{0,1,2:T(8,128)S(1)}, f32[81,16,1]{0,1,2:T(8,128)S(1)}, u32[]{:S(2)}, u32[]{:S(2)}) collective-permute-start(f32[81,16,1]{0,1,2:T(8,128)S(1)} %copy.30), channel_id=1, source_target_pairs={{0,1},{1,2},{2,3},{3,4},{4,5},{5,6},{6,7},{7,0},{8,9},{9,10},{10,1... | collective-permute-start | bytes 15560 | tf_op jit(solution)/shard_map/while/body/eval_jaxpr/ppermute | solution.py:23
  26.9 5.3 %collective-permute-start.1 = (f32[81,16,1]{0,1,2:T(8,128)S(1)}, f32[81,16,1]{0,1,2:T(8,128)S(1)}, u32[]{:S(2)}, u32[]{:S(2)}) collective-permute-start(f32[81,16,1]{0,1,2:T(8,128)S(1)} %copy.32), channel_id=1, source_target_pairs={{1,0},{2,1},{3,2},{4,3},{5,4},{6,5},{7,6},{0,7},{9,8},{10,9},{11,1... | collective-permute-start | bytes 15560 | tf_op jit(solution)/shard_map/while/body/eval_jaxpr/ppermute | solution.py:25
  33.2 5.4 %collective-permute-start.2 = (f32[81,1,130]{2,1,0:T(1,128)S(1)}, f32[81,1,130]{2,1,0:T(1,128)S(1)}, u32[]{:S(2)}, u32[]{:S(2)}) collective-permute-start(f32[81,1,130]{2,1,0:T(1,128)S(1)} %get-tuple-element.386), channel_id=1, source_target_pairs={{0,8},{8,16},{16,24},{1,9},{9,17},{17,25},{2,10},{10,18},{18,26},{... | collective-permute-start | bytes 126368 | tf_op jit(solution)/shard_map/while/body/eval_jaxpr/ppermute | solution.py:23
  37.2 3.6 %collective-permute-start.3 = (f32[81,1,130]{2,1,0:T(1,128)S(1)}, f32[81,1,130]{2,1,0:T(1,128)S(1)}, u32[]{:S(2)}, u32[]{:S(2)}) collective-permute-start(f32[81,1,130]{2,1,0:T(1,128)S(1)} %get-tuple-element.387), channel_id=1, source_target_pairs={{8,0},{16,8},{24,16},{9,1},{17,9},{25,17},{10,2},{18,10},{26,18},{... | collective-permute-start | bytes 126368 | tf_op jit(solution)/shard_map/while/body/eval_jaxpr/ppermute | solution.py:25
  44.5 6.4 %collective-permute-start = (f32[81,16,1]{0,1,2:T(8,128)S(1)}, f32[81,16,1]{0,1,2:T(8,128)S(1)}, u32[]{:S(2)}, u32[]{:S(2)}) collective-permute-start(f32[81,16,1]{0,1,2:T(8,128)S(1)} %copy.30), channel_id=1, source_target_pairs={{0,1},{1,2},{2,3},{3,4},{4,5},{5,6},{6,7},{7,0},{8,9},{9,10},{10,1... | collective-permute-start | bytes 15560 | tf_op jit(solution)/shard_map/while/body/eval_jaxpr/ppermute | solution.py:23
  44.9 6.4 %collective-permute-start.1 = (f32[81,16,1]{0,1,2:T(8,128)S(1)}, f32[81,16,1]{0,1,2:T(8,128)S(1)}, u32[]{:S(2)}, u32[]{:S(2)}) collective-permute-start(f32[81,16,1]{0,1,2:T(8,128)S(1)} %copy.32), channel_id=1, source_target_pairs={{1,0},{2,1},{3,2},{4,3},{5,4},{6,5},{7,6},{0,7},{9,8},{10,9},{11,1... | collective-permute-start | bytes 15560 | tf_op jit(solution)/shard_map/while/body/eval_jaxpr/ppermute | solution.py:25
  52.3 5.4 %collective-permute-start.2 = (f32[81,1,130]{2,1,0:T(1,128)S(1)}, f32[81,1,130]{2,1,0:T(1,128)S(1)}, u32[]{:S(2)}, u32[]{:S(2)}) collective-permute-start(f32[81,1,130]{2,1,0:T(1,128)S(1)} %get-tuple-element.386), channel_id=1, source_target_pairs={{0,8},{8,16},{16,24},{1,9},{9,17},{17,25},{2,10},{10,18},{18,26},{... | collective-permute-start | bytes 126368 | tf_op jit(solution)/shard_map/while/body/eval_jaxpr/ppermute | solution.py:23
  56.4 3.6 %collective-permute-start.3 = (f32[81,1,130]{2,1,0:T(1,128)S(1)}, f32[81,1,130]{2,1,0:T(1,128)S(1)}, u32[]{:S(2)}, u32[]{:S(2)}) collective-permute-start(f32[81,1,130]{2,1,0:T(1,128)S(1)} %get-tuple-element.387), channel_id=1, source_target_pairs={{8,0},{16,8},{24,16},{9,1},{17,9},{25,17},{10,2},{18,10},{26,18},{... | collective-permute-start | bytes 126368 | tf_op jit(solution)/shard_map/while/body/eval_jaxpr/ppermute | solution.py:25
  63.7 6.4 %collective-permute-start = (f32[81,16,1]{0,1,2:T(8,128)S(1)}, f32[81,16,1]{0,1,2:T(8,128)S(1)}, u32[]{:S(2)}, u32[]{:S(2)}) collective-permute-start(f32[81,16,1]{0,1,2:T(8,128)S(1)} %copy.30), channel_id=1, source_target_pairs={{0,1},{1,2},{2,3},{3,4},{4,5},{5,6},{6,7},{7,0},{8,9},{9,10},{10,1... | collective-permute-start | bytes 15560 | tf_op jit(solution)/shard_map/while/body/eval_jaxpr/ppermute | solution.py:23
  64.1 6.4 %collective-permute-start.1 = (f32[81,16,1]{0,1,2:T(8,128)S(1)}, f32[81,16,1]{0,1,2:T(8,128)S(1)}, u32[]{:S(2)}, u32[]{:S(2)}) collective-permute-start(f32[81,16,1]{0,1,2:T(8,128)S(1)} %copy.32), channel_id=1, source_target_pairs={{1,0},{2,1},{3,2},{4,3},{5,4},{6,5},{7,6},{0,7},{9,8},{10,9},{11,1... | collective-permute-start | bytes 15560 | tf_op jit(solution)/shard_map/while/body/eval_jaxpr/ppermute | solution.py:25
  71.5 5.4 %collective-permute-start.2 = (f32[81,1,130]{2,1,0:T(1,128)S(1)}, f32[81,1,130]{2,1,0:T(1,128)S(1)}, u32[]{:S(2)}, u32[]{:S(2)}) collective-permute-start(f32[81,1,130]{2,1,0:T(1,128)S(1)} %get-tuple-element.386), channel_id=1, source_target_pairs={{0,8},{8,16},{16,24},{1,9},{9,17},{17,25},{2,10},{10,18},{18,26},{... | collective-permute-start | bytes 126368 | tf_op jit(solution)/shard_map/while/body/eval_jaxpr/ppermute | solution.py:23
  75.6 3.6 %collective-permute-start.3 = (f32[81,1,130]{2,1,0:T(1,128)S(1)}, f32[81,1,130]{2,1,0:T(1,128)S(1)}, u32[]{:S(2)}, u32[]{:S(2)}) collective-permute-start(f32[81,1,130]{2,1,0:T(1,128)S(1)} %get-tuple-element.387), channel_id=1, source_target_pairs={{8,0},{16,8},{24,16},{9,1},{17,9},{25,17},{10,2},{18,10},{26,18},{... | collective-permute-start | bytes 126368 | tf_op jit(solution)/shard_map/while/body/eval_jaxpr/ppermute | solution.py:25
  82.9 6.4 %collective-permute-start = (f32[81,16,1]{0,1,2:T(8,128)S(1)}, f32[81,16,1]{0,1,2:T(8,128)S(1)}, u32[]{:S(2)}, u32[]{:S(2)}) collective-permute-start(f32[81,16,1]{0,1,2:T(8,128)S(1)} %copy.30), channel_id=1, source_target_pairs={{0,1},{1,2},{2,3},{3,4},{4,5},{5,6},{6,7},{7,0},{8,9},{9,10},{10,1... | collective-permute-start | bytes 15560 | tf_op jit(solution)/shard_map/while/body/eval_jaxpr/ppermute | solution.py:23
  83.2 6.4 %collective-permute-start.1 = (f32[81,16,1]{0,1,2:T(8,128)S(1)}, f32[81,16,1]{0,1,2:T(8,128)S(1)}, u32[]{:S(2)}, u32[]{:S(2)}) collective-permute-start(f32[81,16,1]{0,1,2:T(8,128)S(1)} %copy.32), channel_id=1, source_target_pairs={{1,0},{2,1},{3,2},{4,3},{5,4},{6,5},{7,6},{0,7},{9,8},{10,9},{11,1... | collective-permute-start | bytes 15560 | tf_op jit(solution)/shard_map/while/body/eval_jaxpr/ppermute | solution.py:25
  90.6 5.4 %collective-permute-start.2 = (f32[81,1,130]{2,1,0:T(1,128)S(1)}, f32[81,1,130]{2,1,0:T(1,128)S(1)}, u32[]{:S(2)}, u32[]{:S(2)}) collective-permute-start(f32[81,1,130]{2,1,0:T(1,128)S(1)} %get-tuple-element.386), channel_id=1, source_target_pairs={{0,8},{8,16},{16,24},{1,9},{9,17},{17,25},{2,10},{10,18},{18,26},{... | collective-permute-start | bytes 126368 | tf_op jit(solution)/shard_map/while/body/eval_jaxpr/ppermute | solution.py:23
  94.7 3.6 %collective-permute-start.3 = (f32[81,1,130]{2,1,0:T(1,128)S(1)}, f32[81,1,130]{2,1,0:T(1,128)S(1)}, u32[]{:S(2)}, u32[]{:S(2)}) collective-permute-start(f32[81,1,130]{2,1,0:T(1,128)S(1)} %get-tuple-element.387), channel_id=1, source_target_pairs={{8,0},{16,8},{24,16},{9,1},{17,9},{25,17},{10,2},{18,10},{26,18},{... | collective-permute-start | bytes 126368 | tf_op jit(solution)/shard_map/while/body/eval_jaxpr/ppermute | solution.py:25
  102.0 6.4 %collective-permute-start = (f32[81,16,1]{0,1,2:T(8,128)S(1)}, f32[81,16,1]{0,1,2:T(8,128)S(1)}, u32[]{:S(2)}, u32[]{:S(2)}) collective-permute-start(f32[81,16,1]{0,1,2:T(8,128)S(1)} %copy.30), channel_id=1, source_target_pairs={{0,1},{1,2},{2,3},{3,4},{4,5},{5,6},{6,7},{7,0},{8,9},{9,10},{10,1... | collective-permute-start | bytes 15560 | tf_op jit(solution)/shard_map/while/body/eval_jaxpr/ppermute | solution.py:23
  102.4 6.4 %collective-permute-start.1 = (f32[81,16,1]{0,1,2:T(8,128)S(1)}, f32[81,16,1]{0,1,2:T(8,128)S(1)}, u32[]{:S(2)}, u32[]{:S(2)}) collective-permute-start(f32[81,16,1]{0,1,2:T(8,128)S(1)} %copy.32), channel_id=1, source_target_pairs={{1,0},{2,1},{3,2},{4,3},{5,4},{6,5},{7,6},{0,7},{9,8},{10,9},{11,1... | collective-permute-start | bytes 15560 | tf_op jit(solution)/shard_map/while/body/eval_jaxpr/ppermute | solution.py:25
  109.8 5.4 %collective-permute-start.2 = (f32[81,1,130]{2,1,0:T(1,128)S(1)}, f32[81,1,130]{2,1,0:T(1,128)S(1)}, u32[]{:S(2)}, u32[]{:S(2)}) collective-permute-start(f32[81,1,130]{2,1,0:T(1,128)S(1)} %get-tuple-element.386), channel_id=1, source_target_pairs={{0,8},{8,16},{16,24},{1,9},{9,17},{17,25},{2,10},{10,18},{18,26},{... | collective-permute-start | bytes 126368 | tf_op jit(solution)/shard_map/while/body/eval_jaxpr/ppermute | solution.py:23
  113.9 3.6 %collective-permute-start.3 = (f32[81,1,130]{2,1,0:T(1,128)S(1)}, f32[81,1,130]{2,1,0:T(1,128)S(1)}, u32[]{:S(2)}, u32[]{:S(2)}) collective-permute-start(f32[81,1,130]{2,1,0:T(1,128)S(1)} %get-tuple-element.387), channel_id=1, source_target_pairs={{8,0},{16,8},{24,16},{9,1},{17,9},{25,17},{10,2},{18,10},{26,18},{... | collective-permute-start | bytes 126368 | tf_op jit(solution)/shard_map/while/body/eval_jaxpr/ppermute | solution.py:25
  121.2 6.4 %collective-permute-start = (f32[81,16,1]{0,1,2:T(8,128)S(1)}, f32[81,16,1]{0,1,2:T(8,128)S(1)}, u32[]{:S(2)}, u32[]{:S(2)}) collective-permute-start(f32[81,16,1]{0,1,2:T(8,128)S(1)} %copy.30), channel_id=1, source_target_pairs={{0,1},{1,2},{2,3},{3,4},{4,5},{5,6},{6,7},{7,0},{8,9},{9,10},{10,1... | collective-permute-start | bytes 15560 | tf_op jit(solution)/shard_map/while/body/eval_jaxpr/ppermute | solution.py:23
  121.5 6.4 %collective-permute-start.1 = (f32[81,16,1]{0,1,2:T(8,128)S(1)}, f32[81,16,1]{0,1,2:T(8,128)S(1)}, u32[]{:S(2)}, u32[]{:S(2)}) collective-permute-start(f32[81,16,1]{0,1,2:T(8,128)S(1)} %copy.32), channel_id=1, source_target_pairs={{1,0},{2,1},{3,2},{4,3},{5,4},{6,5},{7,6},{0,7},{9,8},{10,9},{11,1... | collective-permute-start | bytes 15560 | tf_op jit(solution)/shard_map/while/body/eval_jaxpr/ppermute | solution.py:25
  129.0 5.4 %collective-permute-start.2 = (f32[81,1,130]{2,1,0:T(1,128)S(1)}, f32[81,1,130]{2,1,0:T(1,128)S(1)}, u32[]{:S(2)}, u32[]{:S(2)}) collective-permute-start(f32[81,1,130]{2,1,0:T(1,128)S(1)} %get-tuple-element.386), channel_id=1, source_target_pairs={{0,8},{8,16},{16,24},{1,9},{9,17},{17,25},{2,10},{10,18},{18,26},{... | collective-permute-start | bytes 126368 | tf_op jit(solution)/shard_map/while/body/eval_jaxpr/ppermute | solution.py:23
  133.0 3.6 %collective-permute-start.3 = (f32[81,1,130]{2,1,0:T(1,128)S(1)}, f32[81,1,130]{2,1,0:T(1,128)S(1)}, u32[]{:S(2)}, u32[]{:S(2)}) collective-permute-start(f32[81,1,130]{2,1,0:T(1,128)S(1)} %get-tuple-element.387), channel_id=1, source_target_pairs={{8,0},{16,8},{24,16},{9,1},{17,9},{25,17},{10,2},{18,10},{26,18},{... | collective-permute-start | bytes 126368 | tf_op jit(solution)/shard_map/while/body/eval_jaxpr/ppermute | solution.py:25
  140.3 6.4 %collective-permute-start = (f32[81,16,1]{0,1,2:T(8,128)S(1)}, f32[81,16,1]{0,1,2:T(8,128)S(1)}, u32[]{:S(2)}, u32[]{:S(2)}) collective-permute-start(f32[81,16,1]{0,1,2:T(8,128)S(1)} %copy.30), channel_id=1, source_target_pairs={{0,1},{1,2},{2,3},{3,4},{4,5},{5,6},{6,7},{7,0},{8,9},{9,10},{10,1... | collective-permute-start | bytes 15560 | tf_op jit(solution)/shard_map/while/body/eval_jaxpr/ppermute | solution.py:23
  140.7 6.4 %collective-permute-start.1 = (f32[81,16,1]{0,1,2:T(8,128)S(1)}, f32[81,16,1]{0,1,2:T(8,128)S(1)}, u32[]{:S(2)}, u32[]{:S(2)}) collective-permute-start(f32[81,16,1]{0,1,2:T(8,128)S(1)} %copy.32), channel_id=1, source_target_pairs={{1,0},{2,1},{3,2},{4,3},{5,4},{6,5},{7,6},{0,7},{9,8},{10,9},{11,1... | collective-permute-start | bytes 15560 | tf_op jit(solution)/shard_map/while/body/eval_jaxpr/ppermute | solution.py:25
  148.1 5.4 %collective-permute-start.2 = (f32[81,1,130]{2,1,0:T(1,128)S(1)}, f32[81,1,130]{2,1,0:T(1,128)S(1)}, u32[]{:S(2)}, u32[]{:S(2)}) collective-permute-start(f32[81,1,130]{2,1,0:T(1,128)S(1)} %get-tuple-element.386), channel_id=1, source_target_pairs={{0,8},{8,16},{16,24},{1,9},{9,17},{17,25},{2,10},{10,18},{18,26},{... | collective-permute-start | bytes 126368 | tf_op jit(solution)/shard_map/while/body/eval_jaxpr/ppermute | solution.py:23
  152.2 3.6 %collective-permute-start.3 = (f32[81,1,130]{2,1,0:T(1,128)S(1)}, f32[81,1,130]{2,1,0:T(1,128)S(1)}, u32[]{:S(2)}, u32[]{:S(2)}) collective-permute-start(f32[81,1,130]{2,1,0:T(1,128)S(1)} %get-tuple-element.387), channel_id=1, source_target_pairs={{8,0},{16,8},{24,16},{9,1},{17,9},{25,17},{10,2},{18,10},{26,18},{... | collective-permute-start | bytes 126368 | tf_op jit(solution)/shard_map/while/body/eval_jaxpr/ppermute | solution.py:25
  159.5 6.4 %collective-permute-start = (f32[81,16,1]{0,1,2:T(8,128)S(1)}, f32[81,16,1]{0,1,2:T(8,128)S(1)}, u32[]{:S(2)}, u32[]{:S(2)}) collective-permute-start(f32[81,16,1]{0,1,2:T(8,128)S(1)} %copy.30), channel_id=1, source_target_pairs={{0,1},{1,2},{2,3},{3,4},{4,5},{5,6},{6,7},{7,0},{8,9},{9,10},{10,1... | collective-permute-start | bytes 15560 | tf_op jit(solution)/shard_map/while/body/eval_jaxpr/ppermute | solution.py:23
  159.9 6.4 %collective-permute-start.1 = (f32[81,16,1]{0,1,2:T(8,128)S(1)}, f32[81,16,1]{0,1,2:T(8,128)S(1)}, u32[]{:S(2)}, u32[]{:S(2)}) collective-permute-start(f32[81,16,1]{0,1,2:T(8,128)S(1)} %copy.32), channel_id=1, source_target_pairs={{1,0},{2,1},{3,2},{4,3},{5,4},{6,5},{7,6},{0,7},{9,8},{10,9},{11,1... | collective-permute-start | bytes 15560 | tf_op jit(solution)/shard_map/while/body/eval_jaxpr/ppermute | solution.py:25
  167.3 5.4 %collective-permute-start.2 = (f32[81,1,130]{2,1,0:T(1,128)S(1)}, f32[81,1,130]{2,1,0:T(1,128)S(1)}, u32[]{:S(2)}, u32[]{:S(2)}) collective-permute-start(f32[81,1,130]{2,1,0:T(1,128)S(1)} %get-tuple-element.386), channel_id=1, source_target_pairs={{0,8},{8,16},{16,24},{1,9},{9,17},{17,25},{2,10},{10,18},{18,26},{... | collective-permute-start | bytes 126368 | tf_op jit(solution)/shard_map/while/body/eval_jaxpr/ppermute | solution.py:23
  171.4 3.6 %collective-permute-start.3 = (f32[81,1,130]{2,1,0:T(1,128)S(1)}, f32[81,1,130]{2,1,0:T(1,128)S(1)}, u32[]{:S(2)}, u32[]{:S(2)}) collective-permute-start(f32[81,1,130]{2,1,0:T(1,128)S(1)} %get-tuple-element.387), channel_id=1, source_target_pairs={{8,0},{16,8},{24,16},{9,1},{17,9},{25,17},{10,2},{18,10},{26,18},{... | collective-permute-start | bytes 126368 | tf_op jit(solution)/shard_map/while/body/eval_jaxpr/ppermute | solution.py:25
  178.7 6.4 %collective-permute-start = (f32[81,16,1]{0,1,2:T(8,128)S(1)}, f32[81,16,1]{0,1,2:T(8,128)S(1)}, u32[]{:S(2)}, u32[]{:S(2)}) collective-permute-start(f32[81,16,1]{0,1,2:T(8,128)S(1)} %copy.30), channel_id=1, source_target_pairs={{0,1},{1,2},{2,3},{3,4},{4,5},{5,6},{6,7},{7,0},{8,9},{9,10},{10,1... | collective-permute-start | bytes 15560 | tf_op jit(solution)/shard_map/while/body/eval_jaxpr/ppermute | solution.py:23
  179.0 6.4 %collective-permute-start.1 = (f32[81,16,1]{0,1,2:T(8,128)S(1)}, f32[81,16,1]{0,1,2:T(8,128)S(1)}, u32[]{:S(2)}, u32[]{:S(2)}) collective-permute-start(f32[81,16,1]{0,1,2:T(8,128)S(1)} %copy.32), channel_id=1, source_target_pairs={{1,0},{2,1},{3,2},{4,3},{5,4},{6,5},{7,6},{0,7},{9,8},{10,9},{11,1... | collective-permute-start | bytes 15560 | tf_op jit(solution)/shard_map/while/body/eval_jaxpr/ppermute | solution.py:25
  186.4 5.4 %collective-permute-start.2 = (f32[81,1,130]{2,1,0:T(1,128)S(1)}, f32[81,1,130]{2,1,0:T(1,128)S(1)}, u32[]{:S(2)}, u32[]{:S(2)}) collective-permute-start(f32[81,1,130]{2,1,0:T(1,128)S(1)} %get-tuple-element.386), channel_id=1, source_target_pairs={{0,8},{8,16},{16,24},{1,9},{9,17},{17,25},{2,10},{10,18},{18,26},{... | collective-permute-start | bytes 126368 | tf_op jit(solution)/shard_map/while/body/eval_jaxpr/ppermute | solution.py:23
  190.5 3.6 %collective-permute-start.3 = (f32[81,1,130]{2,1,0:T(1,128)S(1)}, f32[81,1,130]{2,1,0:T(1,128)S(1)}, u32[]{:S(2)}, u32[]{:S(2)}) collective-permute-start(f32[81,1,130]{2,1,0:T(1,128)S(1)} %get-tuple-element.387), channel_id=1, source_target_pairs={{8,0},{16,8},{24,16},{9,1},{17,9},{25,17},{10,2},{18,10},{26,18},{... | collective-permute-start | bytes 126368 | tf_op jit(solution)/shard_map/while/body/eval_jaxpr/ppermute | solution.py:25
  196.2 57.6 %copy-start = (s32[8,32,1024]{2,1,0:T(8,128)S(1)}, s32[8,32,1024]{2,1,0:T(8,128)}, u32[]{:S(2)}) copy-start(s32[8,32,1024]{2,1,0:T(8,128)} %param.19) | copy-start | bytes 3145732
  253.8 6.8 %copy-start.5 = (f32[20,4,16,128]{3,2,1,0:T(8,128)}, f32[20,4,16,128]{3,2,1,0:T(8,128)S(1)}, u32[]{:S(2)}) copy-start(f32[20,4,16,128]{3,2,1,0:T(8,128)S(1)} %get-tuple-element.168) | copy-start | bytes 1966084
  276.0 0.9 copy-start.2
  276.0 0.9 copy-start.3
  276.0 0.9 copy-start.4
  (2 other events, 1.7 us)

commit v2 on v1

--- a/solution.py
+++ b/solution.py
@@ -12,58 +12,162 @@
 SUB = 8
 
 
-def with_halo(cells, sides, width, closed):
-    for axis, dim in sides:
-        count = lax.axis_size(axis)
-        ends = count if closed else count - 1
-        head = lax.slice_in_dim(cells, 0, width, axis=dim)
-        tail = lax.slice_in_dim(cells, cells.shape[dim] - width, cells.shape[dim], axis=dim)
-        cells = jnp.concatenate(
-            [
-                lax.ppermute(tail, axis, [(i, (i + 1) % count) for i in range(ends)]),
-                cells,
-                lax.ppermute(head, axis, [((i + 1) % count, i) for i in range(ends)]),
-            ],
-            axis=dim,
+def lane_ids():
+    return lax.broadcasted_iota(jnp.int32, (SUB, LANES), 1)
+
+
+def lay_kernel(rows, layers, field_ref, kappa_ref, mask_ref, out_ref):
+    wide = layers + SUB
+    coef = kappa_ref[...] * mask_ref[...].astype(jnp.float32)
+    for r in range(rows):
+        for g in range(layers // SUB):
+            out_ref[pl.ds(r * wide + g * SUB, SUB), :] = field_ref[
+                pl.ds(g * SUB * rows + r, SUB, stride=rows), :
+            ]
+        out_ref[pl.ds(r * wide + layers, SUB), :] = jnp.broadcast_to(
+            coef[r : r + 1, :], (SUB, LANES)
         )
-    return cells
-
-
-def diffuse_step(wide, gwide):
-    centre = wide[:, 1:-1, 1:-1]
-    flux = gwide[2:, 1:-1] * (wide[:, 2:, 1:-1] - centre)
-    flux = flux + gwide[:-2, 1:-1] * (wide[:, :-2, 1:-1] - centre)
-    flux = flux + gwide[1:-1, 2:] * (wide[:, 1:-1, 2:] - centre)
-    flux = flux + gwide[1:-1, :-2] * (wide[:, 1:-1, :-2] - centre)
-    return centre + gwide[1:-1, 1:-1] * flux
-
-
-def column_solve(rhs, vert_coef):
-    upper_coef = jnp.concatenate([vert_coef[1:], jnp.zeros_like(vert_coef[:1])], axis=0)
-    diag = 1.0 + vert_coef + upper_coef
-    lower = -vert_coef
-    upper = -upper_coef
-
-    def forward(carry, items):
-        cprev, dprev = carry
-        low, mid, up, right = items
-        denom = mid - low * cprev
-        cnew = up / denom
-        dnew = (right - low[None] * dprev) / denom[None]
-        return ((cnew, dnew), (cnew, dnew))
-
-    init = (jnp.zeros(rhs.shape[2:], jnp.float32), jnp.zeros(rhs.shape[1:], jnp.float32))
-    _, (cstore, dstore) = lax.scan(forward, init, (lower, diag, upper, rhs))
-
-    def backward(ynext, items):
-        cval, dval = items
-        yval = dval - cval[None] * ynext
-        return (yval, yval)
-
-    _, result = lax.scan(
-        backward, jnp.zeros(rhs.shape[1:], jnp.float32), (cstore, dstore), reverse=True
-    )
-    return result
+
+
+def pack_kernel(rows, groups, main_ref, north_ref, south_ref, head_ref, tail_ref):
+    lane = lane_ids()
+    pitch = LANES // groups
+    wide = groups * SUB
+
+    def pack(src, count, start):
+        def one_row(r, carry):
+            base = pl.multiple_of(r * wide, SUB)
+            head = jnp.zeros((SUB, LANES), jnp.float32)
+            tail = head
+            for g in range(groups):
+                cells = src[pl.ds(base + g * SUB, SUB), :]
+                spot = (lane >= g * pitch) & (lane < g * pitch + STEPS)
+                head = jnp.where(spot, pltpu.roll(cells, g * pitch, 1), head)
+                move = (g * pitch + STEPS) % LANES
+                tail = jnp.where(spot, pltpu.roll(cells, move, 1), tail)
+            at = pl.ds(pl.multiple_of((start + r) * SUB, SUB), SUB)
+            head_ref[at, :] = head
+            tail_ref[at, :] = tail
+            return carry
+
+        lax.fori_loop(0, count, one_row, 0)
+
+    pack(north_ref, STEPS, 0)
+    pack(main_ref, rows, STEPS)
+    pack(south_ref, STEPS, STEPS + rows)
+
+
+def diffuse(rows, layers, main_ref, north_ref, south_ref, west_ref, east_ref, near, far, coefs):
+    lane = lane_ids()
+    groups = layers // SUB + 1
+    pitch = LANES // groups
+    wide = groups * SUB
+    tall = rows + 2 * STEPS
+
+    def outer(r, g):
+        at = pl.ds(pl.multiple_of(r * SUB, SUB), SUB)
+        east = pltpu.roll(east_ref[at, :], (LANES - g * pitch) % LANES, 1)
+        west = pltpu.roll(west_ref[at, :], (2 * LANES - STEPS - g * pitch) % LANES, 1)
+        return jnp.where(lane < STEPS, east, jnp.where(lane >= LANES - STEPS, west, 0.0))
+
+    def fill(src, count, start):
+        def one_row(r, carry):
+            base = pl.multiple_of(r * wide, SUB)
+            row = start + r
+            for g in range(groups - 1):
+                at = pl.ds(pl.multiple_of(row * layers + g * SUB, SUB), SUB)
+                near[0, at, :] = src[pl.ds(base + g * SUB, SUB), :]
+                far[0, at, :] = outer(row, g)
+            at = pl.ds(pl.multiple_of(row * SUB, SUB), SUB)
+            coefs[10, at, :] = src[pl.ds(base + layers, SUB), :]
+            coefs[11, at, :] = outer(row, groups - 1)
+            return carry
+
+        lax.fori_loop(0, count, one_row, 0)
+
+    fill(north_ref, STEPS, 0)
+    fill(main_ref, rows, STEPS)
+    fill(south_ref, STEPS, STEPS + rows)
+
+    def sides(a, b):
+        ra, rb = pltpu.roll(a, 1, 1), pltpu.roll(b, 1, 1)
+        la, lb = pltpu.roll(a, LANES - 1, 1), pltpu.roll(b, LANES - 1, 1)
+        first, last = lane == 0, lane == LANES - 1
+        return (
+            (jnp.where(first, rb, ra), jnp.where(last, lb, la)),
+            (jnp.where(first, ra, rb), jnp.where(last, la, lb)),
+        )
+
+    def weigh(r, carry):
+        at = pl.ds(pl.multiple_of(r * SUB, SUB), SUB)
+        up = pl.ds(pl.multiple_of((r - 1) * SUB, SUB), SUB)
+        down = pl.ds(pl.multiple_of((r + 1) * SUB, SUB), SUB)
+        both = sides(coefs[10, at, :], coefs[11, at, :])
+        for k in range(2):
+            here = coefs[10 + k, at, :]
+            n = here * coefs[10 + k, up, :]
+            s = here * coefs[10 + k, down, :]
+            w = here * both[k][0]
+            e = here * both[k][1]
+            coefs[5 * k, at, :] = 1.0 - ((n + s) + (w + e))
+            coefs[5 * k + 1, at, :] = n
+            coefs[5 * k + 2, at, :] = s
+            coefs[5 * k + 3, at, :] = w
+            coefs[5 * k + 4, at, :] = e
+        return carry
+
+    lax.fori_loop(1, tall - 1, weigh, 0)
+
+    for step in range(STEPS):
+        now, later = step % 2, (step + 1) % 2
+
+        def one_row(r, carry, now=now, later=later):
+            at = pl.ds(pl.multiple_of(r * SUB, SUB), SUB)
+            c = [coefs[k, at, :] for k in range(10)]
+            for g in range(groups - 1):
+                mid = pl.ds(pl.multiple_of(r * layers + g * SUB, SUB), SUB)
+                up = pl.ds(pl.multiple_of((r - 1) * layers + g * SUB, SUB), SUB)
+                down = pl.ds(pl.multiple_of((r + 1) * layers + g * SUB, SUB), SUB)
+                a, b = near[now, mid, :], far[now, mid, :]
+                both = sides(a, b)
+                for k, (buf, cells) in enumerate(((near, a), (far, b))):
+                    p = c[5 * k : 5 * k + 5]
+                    total = p[0] * cells + p[1] * buf[now, up, :]
+                    other = p[3] * both[k][0] + p[4] * both[k][1]
+                    buf[later, mid, :] = (total + p[2] * buf[now, down, :]) + other
+            return carry
+
+        lax.fori_loop(step + 1, tall - 1 - step, one_row, 0)
+
+
+def solve_columns(rows, layers, near, vert_ref, inc_ref):
+    levels = vert_ref.shape[0] // rows
+    fields = layers // levels
+    done = STEPS % 2
+    for h in range(rows // SUB):
+        ratio = []
+        coef = vert_ref[pl.ds(h * SUB, SUB), :]
+        cprev = jnp.zeros((SUB, LANES), jnp.float32)
+        prev = [cprev] * fields
+        for k in range(levels):
+            if k + 1 < levels:
+                below = vert_ref[pl.ds((k + 1) * rows + h * SUB, SUB), :]
+            else:
+                below = jnp.zeros((SUB, LANES), jnp.float32)
+            inv = 1.0 / (((1.0 + coef) + below) + coef * cprev)
+            cprev = -below * inv
+            ratio.append(cprev)
+            for f in range(fields):
+                layer = k * fields + f
+                right = near[done, pl.ds((STEPS + h * SUB) * layers + layer, SUB, stride=layers), :]
+                prev[f] = (right + coef * prev[f]) * inv
+                inc_ref[pl.ds(layer * rows + h * SUB, SUB), :] = prev[f]
+            coef = below
+        for k in range(levels - 2, -1, -1):
+            for f in range(fields):
+                at = pl.ds((k * fields + f) * rows + h * SUB, SUB)
+                prev[f] = inc_ref[at, :] - ratio[k] * prev[f]
+                inc_ref[at, :] = prev[f]
 
 
 def pick(table, row, col):
@@ -76,7 +180,29 @@
     return level[0]
 
 
-def gather_kernel(rows, layers, owners, inc_ref, off_ref, w_ref, out_ref, off_t, w_t, acc):
+def column_kernel(
+    rows,
+    layers,
+    owners,
+    main_ref,
+    north_ref,
+    south_ref,
+    west_ref,
+    east_ref,
+    vert_ref,
+    off_ref,
+    w_ref,
+    inc_ref,
+    out_ref,
+    near,
+    far,
+    coefs,
+    off_t,
+    w_t,
+    acc,
+):
+    diffuse(rows, layers, main_ref, north_ref, south_ref, west_ref, east_ref, near, far, coefs)
+    solve_columns(rows, layers, near, vert_ref, inc_ref)
     cap = off_ref.shape[1]
     groups = off_ref.shape[0] // LANES
     turns = -(-cap // layers)
@@ -114,28 +240,77 @@
         out_ref[:, here] = total
 
 
-def gather_partials(increment, offsets, weights):
-    layers, rows, cols = increment.shape
+def shift(block, axis, step, closed):
+    count = lax.axis_size(axis)
+    pairs = [(i, (i + step) % count) for i in range(count)]
+    if not closed:
+        pairs = [(i, j) for i, j in pairs if j == i + step]
+    return lax.ppermute(block, axis, pairs)
+
+
+def local_call(kernel, shapes, count, scratch=(), name=None):
+    return pl.pallas_call(
+        kernel,
+        out_shape=shapes,
+        in_specs=[pl.BlockSpec(memory_space=pltpu.VMEM)] * count,
+        out_specs=jax.tree.map(lambda _: pl.BlockSpec(memory_space=pltpu.VMEM), shapes),
+        scratch_shapes=list(scratch),
+        compiler_params=pltpu.CompilerParams(vmem_limit_bytes=40 * 1024 * 1024),
+        name=name,
+    )
+
+
+def floats(*shape):
+    return jax.ShapeDtypeStruct(shape, jnp.float32)
+
+
+def columns_and_partials(control, kappa, sea_mask, vert_coef, offsets, weights):
+    levels, fields, rows, cols = control.shape
+    layers = levels * fields
+    groups = layers // SUB + 1
+    wide = groups * SUB
+    tall = rows + 2 * STEPS
     sten, owners, cap = offsets.shape
-    groups = sten * owners // LANES
+    bundles = sten * owners // LANES
     padded = -(-cap // layers) * layers
-    return pl.pallas_call(
-        functools.partial(gather_kernel, rows, layers, owners),
-        out_shape=jax.ShapeDtypeStruct((owners, cap), jnp.float32),
-        in_specs=[pl.BlockSpec(memory_space=pltpu.VMEM)] * 3,
-        out_specs=pl.BlockSpec(memory_space=pltpu.VMEM),
-        scratch_shapes=[
-            pltpu.VMEM((groups, padded, LANES), jnp.int32),
-            pltpu.VMEM((groups, padded, LANES), jnp.float32),
+
+    main = local_call(
+        functools.partial(lay_kernel, rows, layers), floats(rows * wide, LANES), 3, name="lay"
+    )(control.reshape(layers * rows, cols), kappa, sea_mask)
+    north = shift(main[(rows - STEPS) * wide :], "lat", 1, False)
+    south = shift(main[: STEPS * wide], "lat", -1, False)
+    head, tail = local_call(
+        functools.partial(pack_kernel, rows, groups),
+        (floats(tall * SUB, LANES), floats(tall * SUB, LANES)),
+        3,
+        name="pack",
+    )(main, north, south)
+    west = shift(tail, "lon", 1, True)
+    east = shift(head, "lon", -1, True)
+    increment, partial_value = local_call(
+        functools.partial(column_kernel, rows, layers, owners),
+        (floats(layers * rows, LANES), floats(owners, cap)),
+        8,
+        [
+            pltpu.VMEM((2, tall * layers, LANES), jnp.float32),
+            pltpu.VMEM((2, tall * layers, LANES), jnp.float32),
+            pltpu.VMEM((12, tall * SUB, LANES), jnp.float32),
+            pltpu.VMEM((bundles, padded, LANES), jnp.int32),
+            pltpu.VMEM((bundles, padded, LANES), jnp.float32),
             pltpu.VMEM((padded, LANES), jnp.float32),
         ],
-        compiler_params=pltpu.CompilerParams(vmem_limit_bytes=32 * 1024 * 1024),
-        name="gather_partials",
+        name="columns",
     )(
-        increment.reshape(layers * rows, cols),
+        main,
+        north,
+        south,
+        west,
+        east,
+        vert_coef.reshape(levels * rows, cols),
         offsets.reshape(sten * owners, cap),
         weights.reshape(sten * owners, cap),
     )
+    return increment.reshape(control.shape), partial_value
 
 
 def split_parts(v):
@@ -196,24 +371,8 @@
     observed,
     inv_error,
 ):
-    levels, fields, rows, cols = control.shape
-    coef = kappa * sea_mask.astype(jnp.float32)
-    field = control.reshape(levels * fields, rows, cols)
-    depth = 1
-
-    def one_round(turn, state):
-        stacked = jnp.concatenate([state, coef[None]], axis=0)
-        wide = with_halo(stacked, (("lon", 2),), depth, True)
-        wide = with_halo(wide, (("lat", 1),), depth, False)
-        inner = wide[:-1]
-        gwide = wide[-1]
-        inner = diffuse_step(inner, gwide)
-        return inner
-
-    field = lax.fori_loop(0, STEPS // depth, one_round, field)
-    increment = column_solve(field.reshape(levels, fields, rows, cols), vert_coef)
-    partial_value = gather_partials(
-        increment.reshape(levels * fields, rows, cols), stencil_offsets, stencil_weights
+    increment, partial_value = columns_and_partials(
+        control, kappa, sea_mask, vert_coef, stencil_offsets, stencil_weights
     )
     received = lax.all_to_all(
         partial_value, ("lat", "lon"), split_axis=0, concat_axis=0, tiled=True

time: 291 us -> 101 us (0.35); the launches traced: 287 us -> 100 us
  starting transfers between devices: 99.6 us -> 10.7 us
  other arithmetic: 72 us -> 0 us
  Pallas kernels: 16.4 us -> 61.1 us
  local copies, waits for them, and re-layouts: 44.4 us -> 3.59 us
  waiting for transfers between devices: 36.8 us -> 5 us
  blocking collectives: 15.3 us -> 19 us
    ppermute x40 -> x4, starting transfers between devices: 99.6 us -> 10.7 us  [shift(): return lax.ppermute(block, axis, pairs)]
    pallas_call x1 -> x3, Pallas kernels: 6.75 us -> 51.5 us  [the longest x1 48 us: columns_and_partials(): local_call(functools.partial(column_kernel, rows, layers, owners), (float...]
    dynamic_update_slice x60 -> x0, other arithmetic: 42.6 us -> none  [column_solve(): _, (cstore, dstore) = lax.scan(forward, init, (lower, diag, upper, rhs))]
    ppermute x40 -> x4, waiting for transfers between devices: 36.8 us -> 5 us  [shift(): return lax.ppermute(block, axis, pairs)]
    add x10 -> x0, other arithmetic: 19.5 us -> none  [diffuse_step(): return centre + gwide[1:-1, 1:-1] * flux]
    mul x20 -> x0, local copies, waits for them, and re-layouts: 14.1 us -> none  [backward(): yval = dval - cval[None] * ynext]
    while x10 -> x0, local copies, waits for them, and re-layouts: 11 us -> none
    concatenate x20 -> x0, other arithmetic: 8.26 us -> none  [the longest x10 5.9 us: with_halo(): jnp.concatenate([lax.ppermute(tail, axis, [(i, (i + 1) % count) for i in...]
  transfers between devices with their start and end apart: 40 -> 4, of which waited for: 20 -> 3; matrix products, arithmetic and copies ran while one was open for 3% -> 0% of each run, Pallas kernels for 0% -> 0%
where the time goes in v2:
time: 101 us; the launch traced here: 100 us
  Pallas kernels  61.1 us (60%)
  blocking collectives  19 us (19%)
  starting transfers between devices  10.7 us (11%)
  waiting for transfers between devices  5 us (5%)
  local copies, waits for them, and re-layouts  3.59 us (4%)
    pallas_call x1, Pallas kernels, columns_and_partials(): local_call(functools.partial(column_kernel, rows, layers, owners), (float...  48 us
    all_to_all x1, blocking collectives, per_device(): lax.all_to_all(partial_value, ('lat', 'lon'), split_axis=0, concat_axis=0...  19 us
    ppermute x4, starting transfers between devices, shift(): return lax.ppermute(block, axis, pairs)  10.7 us
    pallas_call x1, Pallas kernels, scatter_misfit(): pl.pallas_call(scatter_kernel, out_shape=jax.ShapeDtypeStruct((high, LANE...  9.66 us
    ppermute x4, waiting for transfers between devices, shift(): return lax.ppermute(block, axis, pairs)  5 us
    unnamed x19, local copies, waits for them, and re-layouts  3.4 us
    pallas_call x1, Pallas kernels, columns_and_partials(): local_call(functools.partial(pack_kernel, rows, groups), (floats(tall * S...  3.27 us
  transfers between devices with their start and end apart: 4, of which 3 were waited for; matrix products, arithmetic and copies ran while one was open for 0% of the time, Pallas kernels for 0%

profile of v2, /device:TPU:0, one launch (start us, length us, event | category | flops | bytes accessed | tf_op | source)
XLA Modules:
  0.0 100.2 jit_solution(6646192283576581447)
XLA Ops:
  0.6 0.0 copy-start.2
  0.6 1.1 %copy-done.2 = f32[20,4,16,128]{3,2,1,0:T(8,128)S(1)} copy-done((f32[20,4,16,128]{3,2,1,0:T(8,128)S(1)}, f32[20,4,16,128]{3,2,1,0:T(8,128)}, u32[]{:S(2)}) %copy-start.2) | copy-done | bytes 655384
  1.7 0.0 copy-start.7
  1.7 0.7 copy-done.7
  2.4 0.0 copy-start.8
  2.4 0.7 copy-done.8
  3.1 0.2 lay.1.main_ref
  3.3 0.0 copy-start.1
  3.3 0.1 fusion
  3.4 0.0 copy-start
  3.4 1.4 %collective-permute-start.1 = (f32[880,128]{1,0:T(8,128)S(1)}, f32[880,128]{1,0:T(8,128)S(1)}, u32[]{:S(2)}, u32[]{:S(2)}) collective-permute-start(f32[880,128]{1,0:T(8,128)S(1)} %get-tuple-element.10), channel_id=1, source_target_pairs={{8,0},{16,8},{24,16},{9,1},{17,9},{25,17},{10,2},{18,10},{26,18},{... | collective-permute-start | bytes 1351688 | tf_op jit(solution)/shard_map/ppermute | solution.py:248
  4.8 0.0 copy-start.3
  4.9 3.2 %collective-permute-start = (f32[880,128]{1,0:T(8,128)S(1)}, f32[880,128]{1,0:T(8,128)S(1)}, u32[]{:S(2)}, u32[]{:S(2)}) collective-permute-start(f32[880,128]{1,0:T(8,128)S(1)} %get-tuple-element.11), channel_id=1, source_target_pairs={{0,8},{8,16},{16,24},{1,9},{9,17},{17,25},{2,10},{10,18},{18,26},{... | collective-permute-start | bytes 1351688 | tf_op jit(solution)/shard_map/ppermute | solution.py:248
  8.1 0.0 collective-permute-done.1.south_ref
  8.1 1.4 %collective-permute-done.north_ref = f32[880,128]{1,0:T(8,128)S(1)} collective-permute-done((f32[880,128]{1,0:T(8,128)S(1)}, f32[880,128]{1,0:T(8,128)S(1)}, u32[]{:S(2)}, u32[]{:S(2)}) %collective-permute-start) | collective-permute-done | bytes 450592 | tf_op jit(solution)/shard_map/ppermute | solution.py:248
  9.4 3.3 %pack.1 = (f32[288,128]{1,0:T(8,128)S(1)}, f32[288,128]{1,0:T(8,128)S(1)}) custom-call(f32[1408,128]{1,0:T(8,128)S(1)} %lay.1.main_ref, f32[880,128]{1,0:T(8,128)S(1)} %collective-permute-done.north_ref, f32[880,128]{1,0:T(8,128)S(1)} %collective-permute-done.1.south_ref), custom_call_target="tpu_custom_call" | custom-call | tf_op jit(solution)/shard_map/pack/pallas_call | solution.py:282
  12.7 3.0 %collective-permute-start.2 = (f32[288,128]{1,0:T(8,128)S(1)}, f32[288,128]{1,0:T(8,128)S(1)}, u32[]{:S(2)}, u32[]{:S(2)}) collective-permute-start(f32[288,128]{1,0:T(8,128)S(1)} %get-tuple-element.6), channel_id=1, source_target_pairs={{0,1},{1,2},{2,3},{3,4},{4,5},{5,6},{6,7},{7,0},{8,9},{9,10},{10,1... | collective-permute-start | bytes 442376 | tf_op jit(solution)/shard_map/ppermute | solution.py:248
  15.7 3.1 %collective-permute-start.3 = (f32[288,128]{1,0:T(8,128)S(1)}, f32[288,128]{1,0:T(8,128)S(1)}, u32[]{:S(2)}, u32[]{:S(2)}) collective-permute-start(f32[288,128]{1,0:T(8,128)S(1)} %get-tuple-element.7), channel_id=1, source_target_pairs={{0,7},{1,0},{2,1},{3,2},{4,3},{5,4},{6,5},{7,6},{8,15},{9,8},{10,9... | collective-permute-start | bytes 442376 | tf_op jit(solution)/shard_map/ppermute | solution.py:248
  18.9 3.2 %collective-permute-done.2.west_ref = f32[288,128]{1,0:T(8,128)S(1)} collective-permute-done((f32[288,128]{1,0:T(8,128)S(1)}, f32[288,128]{1,0:T(8,128)S(1)}, u32[]{:S(2)}, u32[]{:S(2)}) %collective-permute-start.2) | collective-permute-done | bytes 147488 | tf_op jit(solution)/shard_map/ppermute | solution.py:248
  22.0 0.5 collective-permute-done.3.east_ref
  22.5 0.0 copy-done.1
  22.5 0.0 copy-done
  22.5 0.0 copy-done.3
  22.5 48.0 %columns.1 = (f32[1280,128]{1,0:T(8,128)}, f32[32,1024]{1,0:T(8,128)S(1)}) custom-call(f32[1408,128]{1,0:T(8,128)S(1)} %lay.1.main_ref, f32[880,128]{1,0:T(8,128)S(1)} %collective-permute-done.north_ref, f32[880,128]{1,0:T(8,128)S(1)} %collective-permute-done.1.south_ref, f32[288,128]{1,0:T(8,128)S(1)} %collective-permute-done.2.west_ref, ...), custom_call_target="tpu_custom_call" | custom-call | tf_op jit(solution)/shard_map/columns/pallas_call | solution.py:290
  70.5 0.1 copy.11
  70.6 19.0 %all_to_all.11 = f32[32,1,1024]{2,1,0:T(1,128)S(1)} all-to-all(f32[32,1,1024]{2,1,0:T(1,128)S(1)} %copy.11), channel_id=1, replica_groups=mesh['lat'=4,'lon'=8] {'lat','lon'}, dimensions={0} | all-to-all | bytes 262144 | tf_op jit(solution)/shard_map/all_to_all | solution.py:377
  89.7 0.0 copy-start.4
  89.7 0.0 copy-start.5
  89.7 0.0 copy-start.6
  89.7 0.9 copy-done.4
  90.6 0.0 copy-done.5
  90.6 0.0 copy-done.6
  90.6 9.7 %scatter_misfit.1 = f32[64,128]{1,0:T(8,128)} custom-call(f32[32,1024]{1,0:T(8,128)S(1)} %bitcast.15, s32[32,1024]{1,0:T(8,128)S(1)} %copy-done.4, f32[64,128]{1,0:T(8,128)S(1)} %bitcast.18, f32[64,128]{1,0:T(8,128)S(1)} %bitcast.19), custom_call_target="tpu_custom_call" | custom-call | tf_op jit(solution)/shard_map/scatter_misfit/pallas_call | solution.py:351
  (1 shorter events, 0.0 us)
Async XLA Ops:
  0.6 1.1 %copy-start.2 = (f32[20,4,16,128]{3,2,1,0:T(8,128)S(1)}, f32[20,4,16,128]{3,2,1,0:T(8,128)}, u32[]{:S(2)}) copy-start(f32[20,4,16,128]{3,2,1,0:T(8,128)} %param.9) | copy-start | bytes 1966084
  1.7 0.7 copy-start.7
  2.4 0.7 copy-start.8
  3.3 19.1 %copy-start.1 = (f32[8,32,1024]{2,1,0:T(8,128)S(1)}, f32[8,32,1024]{2,1,0:T(8,128)}, u32[]{:S(2)}) copy-start(f32[8,32,1024]{2,1,0:T(8,128)} %param.14) | copy-start | bytes 3145732
  3.4 19.1 %copy-start = (s32[8,32,1024]{2,1,0:T(8,128)S(1)}, s32[8,32,1024]{2,1,0:T(8,128)}, u32[]{:S(2)}) copy-start(s32[8,32,1024]{2,1,0:T(8,128)} %param.13) | copy-start | bytes 3145732
  3.4 4.6 %collective-permute-start.1 = (f32[880,128]{1,0:T(8,128)S(1)}, f32[880,128]{1,0:T(8,128)S(1)}, u32[]{:S(2)}, u32[]{:S(2)}) collective-permute-start(f32[880,128]{1,0:T(8,128)S(1)} %get-tuple-element.10), channel_id=1, source_target_pairs={{8,0},{16,8},{24,16},{9,1},{17,9},{25,17},{10,2},{18,10},{26,18},{... | collective-permute-start | bytes 1351688 | tf_op jit(solution)/shard_map/ppermute | solution.py:248
  4.8 17.6 %copy-start.3 = (f32[20,16,128]{2,1,0:T(8,128)S(1)}, f32[20,16,128]{2,1,0:T(8,128)}, u32[]{:S(2)}) copy-start(f32[20,16,128]{2,1,0:T(8,128)} %param.12) | copy-start | bytes 491524
  4.9 4.6 %collective-permute-start = (f32[880,128]{1,0:T(8,128)S(1)}, f32[880,128]{1,0:T(8,128)S(1)}, u32[]{:S(2)}, u32[]{:S(2)}) collective-permute-start(f32[880,128]{1,0:T(8,128)S(1)} %get-tuple-element.11), channel_id=1, source_target_pairs={{0,8},{8,16},{16,24},{1,9},{9,17},{17,25},{2,10},{10,18},{18,26},{... | collective-permute-start | bytes 1351688 | tf_op jit(solution)/shard_map/ppermute | solution.py:248
  12.7 9.3 %collective-permute-start.2 = (f32[288,128]{1,0:T(8,128)S(1)}, f32[288,128]{1,0:T(8,128)S(1)}, u32[]{:S(2)}, u32[]{:S(2)}) collective-permute-start(f32[288,128]{1,0:T(8,128)S(1)} %get-tuple-element.6), channel_id=1, source_target_pairs={{0,1},{1,2},{2,3},{3,4},{4,5},{5,6},{6,7},{7,0},{8,9},{9,10},{10,1... | collective-permute-start | bytes 442376 | tf_op jit(solution)/shard_map/ppermute | solution.py:248
  15.7 6.7 %collective-permute-start.3 = (f32[288,128]{1,0:T(8,128)S(1)}, f32[288,128]{1,0:T(8,128)S(1)}, u32[]{:S(2)}, u32[]{:S(2)}) collective-permute-start(f32[288,128]{1,0:T(8,128)S(1)} %get-tuple-element.7), channel_id=1, source_target_pairs={{0,7},{1,0},{2,1},{3,2},{4,3},{5,4},{6,5},{7,6},{8,15},{9,8},{10,9... | collective-permute-start | bytes 442376 | tf_op jit(solution)/shard_map/ppermute | solution.py:248
  89.7 0.9 copy-start.4
  89.7 0.9 copy-start.5
  89.7 0.9 copy-start.6

commit v3 on v2

--- a/solution.py
+++ b/solution.py
@@ -50,14 +50,14 @@
             tail_ref[at, :] = tail
             return carry
 
-        lax.fori_loop(0, count, one_row, 0)
+        lax.fori_loop(0, count, one_row, 0, unroll=2)
 
     pack(north_ref, STEPS, 0)
     pack(main_ref, rows, STEPS)
     pack(south_ref, STEPS, STEPS + rows)
 
 
-def diffuse(rows, layers, main_ref, north_ref, south_ref, west_ref, east_ref, near, far, coefs):
+def diffuse(rows, layers, main_ref, north_ref, south_ref, west_ref, east_ref, near, far, near_b, far_b, coefs):
     lane = lane_ids()
     groups = layers // SUB + 1
     pitch = LANES // groups
@@ -76,14 +76,14 @@
             row = start + r
             for g in range(groups - 1):
                 at = pl.ds(pl.multiple_of(row * layers + g * SUB, SUB), SUB)
-                near[0, at, :] = src[pl.ds(base + g * SUB, SUB), :]
-                far[0, at, :] = outer(row, g)
+                near[at, :] = src[pl.ds(base + g * SUB, SUB), :]
+                far[at, :] = outer(row, g)
             at = pl.ds(pl.multiple_of(row * SUB, SUB), SUB)
             coefs[10, at, :] = src[pl.ds(base + layers, SUB), :]
             coefs[11, at, :] = outer(row, groups - 1)
             return carry
 
-        lax.fori_loop(0, count, one_row, 0)
+        lax.fori_loop(0, count, one_row, 0, unroll=2)
 
     fill(north_ref, STEPS, 0)
     fill(main_ref, rows, STEPS)
@@ -116,34 +116,35 @@
             coefs[5 * k + 4, at, :] = e
         return carry
 
-    lax.fori_loop(1, tall - 1, weigh, 0)
+    lax.fori_loop(1, tall - 1, weigh, 0, unroll=2)
 
     for step in range(STEPS):
-        now, later = step % 2, (step + 1) % 2
-
-        def one_row(r, carry, now=now, later=later):
+        old, new = (near, far), (near_b, far_b)
+        if step % 2:
+            old, new = new, old
+
+        def one_row(r, carry, old=old, new=new):
             at = pl.ds(pl.multiple_of(r * SUB, SUB), SUB)
             c = [coefs[k, at, :] for k in range(10)]
             for g in range(groups - 1):
                 mid = pl.ds(pl.multiple_of(r * layers + g * SUB, SUB), SUB)
                 up = pl.ds(pl.multiple_of((r - 1) * layers + g * SUB, SUB), SUB)
                 down = pl.ds(pl.multiple_of((r + 1) * layers + g * SUB, SUB), SUB)
-                a, b = near[now, mid, :], far[now, mid, :]
+                a, b = old[0][mid, :], old[1][mid, :]
                 both = sides(a, b)
-                for k, (buf, cells) in enumerate(((near, a), (far, b))):
+                for k, cells in enumerate((a, b)):
                     p = c[5 * k : 5 * k + 5]
-                    total = p[0] * cells + p[1] * buf[now, up, :]
+                    total = p[0] * cells + p[1] * old[k][up, :]
                     other = p[3] * both[k][0] + p[4] * both[k][1]
-                    buf[later, mid, :] = (total + p[2] * buf[now, down, :]) + other
+                    new[k][mid, :] = (total + p[2] * old[k][down, :]) + other
             return carry
 
-        lax.fori_loop(step + 1, tall - 1 - step, one_row, 0)
-
-
-def solve_columns(rows, layers, near, vert_ref, inc_ref):
+        lax.fori_loop(step + 1, tall - 1 - step, one_row, 0, unroll=2)
+
+
+def solve_columns(rows, layers, done, vert_ref, inc_ref):
     levels = vert_ref.shape[0] // rows
     fields = layers // levels
-    done = STEPS % 2
     for h in range(rows // SUB):
         ratio = []
         coef = vert_ref[pl.ds(h * SUB, SUB), :]
@@ -159,7 +160,7 @@
             ratio.append(cprev)
             for f in range(fields):
                 layer = k * fields + f
-                right = near[done, pl.ds((STEPS + h * SUB) * layers + layer, SUB, stride=layers), :]
+                right = done[pl.ds((STEPS + h * SUB) * layers + layer, SUB, stride=layers), :]
                 prev[f] = (right + coef * prev[f]) * inv
                 inc_ref[pl.ds(layer * rows + h * SUB, SUB), :] = prev[f]
             coef = below
@@ -178,6 +179,21 @@
         level = [jnp.where(odd, level[i + 1], level[i]) for i in range(0, len(level), 2)]
         bit *= 2
     return level[0]
+
+
+def turn_kernel(off_ref, w_ref, off_t, w_t):
+    cap = off_ref.shape[1]
+    groups = off_ref.shape[0] // LANES
+    padded = off_t.shape[1]
+    if padded > cap:
+        for g in range(groups):
+            off_t[g, cap:padded, :] = jnp.zeros((padded - cap, LANES), jnp.int32)
+            w_t[g, cap:padded, :] = jnp.zeros((padded - cap, LANES), jnp.float32)
+    for g in range(groups):
+        for c in range(cap // LANES):
+            here = pl.ds(c * LANES, LANES)
+            off_t[g, here, :] = off_ref[pl.ds(g * LANES, LANES), here].T
+            w_t[g, here, :] = w_ref[pl.ds(g * LANES, LANES), here].T
 
 
 def column_kernel(
@@ -190,32 +206,24 @@
     west_ref,
     east_ref,
     vert_ref,
-    off_ref,
-    w_ref,
+    off_t,
+    w_t,
     inc_ref,
     out_ref,
     near,
     far,
+    near_b,
+    far_b,
     coefs,
-    off_t,
-    w_t,
     acc,
 ):
-    diffuse(rows, layers, main_ref, north_ref, south_ref, west_ref, east_ref, near, far, coefs)
-    solve_columns(rows, layers, near, vert_ref, inc_ref)
-    cap = off_ref.shape[1]
-    groups = off_ref.shape[0] // LANES
+    diffuse(
+        rows, layers, main_ref, north_ref, south_ref, west_ref, east_ref, near, far, near_b, far_b, coefs
+    )
+    solve_columns(rows, layers, near_b if STEPS % 2 else near, vert_ref, inc_ref)
+    cap = out_ref.shape[1]
+    groups = off_t.shape[0]
     turns = -(-cap // layers)
-    padded = turns * layers
-    if padded > cap:
-        for g in range(groups):
-            off_t[g, cap:padded, :] = jnp.zeros((padded - cap, LANES), jnp.int32)
-            w_t[g, cap:padded, :] = jnp.zeros((padded - cap, LANES), jnp.float32)
-    for g in range(groups):
-        for c in range(cap // LANES):
-            here = pl.ds(c * LANES, LANES)
-            off_t[g, here, :] = off_ref[pl.ds(g * LANES, LANES), here].T
-            w_t[g, here, :] = w_ref[pl.ds(g * LANES, LANES), here].T
 
     def one_group(lg, carry):
         base = pl.multiple_of(lg * SUB, SUB)
@@ -230,7 +238,7 @@
             acc[at, :] = total
         return carry
 
-    lax.fori_loop(0, layers // SUB, one_group, 0)
+    lax.fori_loop(0, layers // SUB, one_group, 0, unroll=2)
     for c in range(cap // LANES):
         here = pl.ds(c * LANES, LANES)
         block = acc[here, :].T
@@ -287,16 +295,25 @@
     )(main, north, south)
     west = shift(tail, "lon", 1, True)
     east = shift(head, "lon", -1, True)
+    off_t, w_t = local_call(
+        turn_kernel,
+        (
+            jax.ShapeDtypeStruct((bundles, padded, LANES), jnp.int32),
+            floats(bundles, padded, LANES),
+        ),
+        2,
+        name="turn",
+    )(offsets.reshape(sten * owners, cap), weights.reshape(sten * owners, cap))
     increment, partial_value = local_call(
         functools.partial(column_kernel, rows, layers, owners),
         (floats(layers * rows, LANES), floats(owners, cap)),
         8,
         [
-            pltpu.VMEM((2, tall * layers, LANES), jnp.float32),
-            pltpu.VMEM((2, tall * layers, LANES), jnp.float32),
+            pltpu.VMEM((tall * layers, LANES), jnp.float32),
+            pltpu.VMEM((tall * layers, LANES), jnp.float32),
+            pltpu.VMEM((tall * layers, LANES), jnp.float32),
+            pltpu.VMEM((tall * layers, LANES), jnp.float32),
             pltpu.VMEM((12, tall * SUB, LANES), jnp.float32),
-            pltpu.VMEM((bundles, padded, LANES), jnp.int32),
-            pltpu.VMEM((bundles, padded, LANES), jnp.float32),
             pltpu.VMEM((padded, LANES), jnp.float32),
         ],
         name="columns",
@@ -307,8 +324,8 @@
         west,
         east,
         vert_coef.reshape(levels * rows, cols),
-        offsets.reshape(sten * owners, cap),
-        weights.reshape(sten * owners, cap),
+        off_t,
+        w_t,
     )
     return increment.reshape(control.shape), partial_value
 
@@ -341,7 +358,7 @@
         acc[...] += spread(rec_ref[pl.ds(p, 1), :], tgt_ref[pl.ds(p, 1), :], high)
         return carry
 
-    lax.fori_loop(0, rec_ref.shape[0], one_source, 0)
+    lax.fori_loop(0, rec_ref.shape[0], one_source, 0, unroll=4)
     total = acc[:high] + acc[high : 2 * high] + acc[2 * high :]
     out_ref[...] = (total - obs_ref[...]) * err_ref[...]
 

time: 101 us -> 76.3 us (0.76)
  Pallas kernels: 61.1 us -> 38.5 us
    pallas_call x1, Pallas kernels: 48 us -> 30.3 us  [columns_and_partials(): local_call(functools.partial(column_kernel, rows, layers, owners), (float...]
    pallas_call x1, Pallas kernels: 9.66 us -> 5.4 us  [scatter_misfit(): pl.pallas_call(scatter_kernel, out_shape=jax.ShapeDtypeStruct((high, LANE...]
    pallas_call x1, Pallas kernels: 3.27 us -> 1.99 us  [columns_and_partials(): local_call(functools.partial(pack_kernel, rows, groups), (floats(tall * S...]
  transfers between devices with their start and end apart: 4 -> 4, of which waited for: 3 -> 3; matrix products, arithmetic and copies ran while one was open for 0% -> 0% of each run, Pallas kernels for 0% -> 1%
where the time goes in v3:
time: 76.3 us; the launch traced here: 76 us
  Pallas kernels  38.5 us (50%)
  blocking collectives  19 us (25%)
  starting transfers between devices  10.6 us (14%)
  waiting for transfers between devices  4.38 us (6%)
  local copies, waits for them, and re-layouts  2.72 us (4%)
    pallas_call x1, Pallas kernels, columns_and_partials(): local_call(functools.partial(column_kernel, rows, layers, owners), (float...  30.3 us
    all_to_all x1, blocking collectives, per_device(): lax.all_to_all(partial_value, ('lat', 'lon'), split_axis=0, concat_axis=0...  19 us
    ppermute x4, starting transfers between devices, shift(): return lax.ppermute(block, axis, pairs)  10.6 us
    pallas_call x1, Pallas kernels, scatter_misfit(): pl.pallas_call(scatter_kernel, out_shape=jax.ShapeDtypeStruct((high, LANE...  5.4 us
    ppermute x4, waiting for transfers between devices, shift(): return lax.ppermute(block, axis, pairs)  4.38 us
    unnamed x19, local copies, waits for them, and re-layouts  2.53 us
    pallas_call x1, Pallas kernels, columns_and_partials(): local_call(functools.partial(pack_kernel, rows, groups), (floats(tall * S...  1.99 us
  transfers between devices with their start and end apart: 4, of which 3 were waited for; matrix products, arithmetic and copies ran while one was open for 0% of the time, Pallas kernels for 1%

profile of v3, /device:TPU:0, one launch (start us, length us, event | category | flops | bytes accessed | tf_op | source)
XLA Modules:
  0.0 76.0 jit_solution(4788594836652264257)
XLA Ops:
  0.6 0.0 copy-start.2
  0.6 1.1 %copy-done.2 = f32[20,4,16,128]{3,2,1,0:T(8,128)S(1)} copy-done((f32[20,4,16,128]{3,2,1,0:T(8,128)S(1)}, f32[20,4,16,128]{3,2,1,0:T(8,128)}, u32[]{:S(2)}) %copy-start.2) | copy-done | bytes 655384
  1.7 0.0 copy-start.7
  1.7 0.7 copy-done.7
  2.4 0.0 copy-start.8
  2.4 0.7 copy-done.8
  3.1 0.2 lay.1.main_ref
  3.3 0.0 copy-start.1
  3.3 0.1 fusion
  3.4 0.0 copy-start
  3.4 1.4 %collective-permute-start.1 = (f32[880,128]{1,0:T(8,128)S(1)}, f32[880,128]{1,0:T(8,128)S(1)}, u32[]{:S(2)}, u32[]{:S(2)}) collective-permute-start(f32[880,128]{1,0:T(8,128)S(1)} %get-tuple-element.14), channel_id=1, source_target_pairs={{8,0},{16,8},{24,16},{9,1},{17,9},{25,17},{10,2},{18,10},{26,18},{... | collective-permute-start | bytes 1351688 | tf_op jit(solution)/shard_map/ppermute | solution.py:256
  4.8 3.1 %collective-permute-start = (f32[880,128]{1,0:T(8,128)S(1)}, f32[880,128]{1,0:T(8,128)S(1)}, u32[]{:S(2)}, u32[]{:S(2)}) collective-permute-start(f32[880,128]{1,0:T(8,128)S(1)} %get-tuple-element.15), channel_id=1, source_target_pairs={{0,8},{8,16},{16,24},{1,9},{9,17},{17,25},{2,10},{10,18},{18,26},{... | collective-permute-start | bytes 1351688 | tf_op jit(solution)/shard_map/ppermute | solution.py:256
  7.9 0.0 collective-permute-done.1.south_ref
  7.9 1.4 %collective-permute-done.north_ref = f32[880,128]{1,0:T(8,128)S(1)} collective-permute-done((f32[880,128]{1,0:T(8,128)S(1)}, f32[880,128]{1,0:T(8,128)S(1)}, u32[]{:S(2)}, u32[]{:S(2)}) %collective-permute-start) | collective-permute-done | bytes 450592 | tf_op jit(solution)/shard_map/ppermute | solution.py:256
  9.3 2.0 %pack.1 = (f32[288,128]{1,0:T(8,128)S(1)}, f32[288,128]{1,0:T(8,128)S(1)}) custom-call(f32[1408,128]{1,0:T(8,128)S(1)} %lay.1.main_ref, f32[880,128]{1,0:T(8,128)S(1)} %collective-permute-done.north_ref, f32[880,128]{1,0:T(8,128)S(1)} %collective-permute-done.1.south_ref), custom_call_target="tpu_custom_call" | custom-call | tf_op jit(solution)/shard_map/pack/pallas_call | solution.py:290
  11.3 0.0 copy-start.3
  11.3 3.0 %collective-permute-start.2 = (f32[288,128]{1,0:T(8,128)S(1)}, f32[288,128]{1,0:T(8,128)S(1)}, u32[]{:S(2)}, u32[]{:S(2)}) collective-permute-start(f32[288,128]{1,0:T(8,128)S(1)} %get-tuple-element.8), channel_id=1, source_target_pairs={{0,1},{1,2},{2,3},{3,4},{4,5},{5,6},{6,7},{7,0},{8,9},{9,10},{10,1... | collective-permute-start | bytes 442376 | tf_op jit(solution)/shard_map/ppermute | solution.py:256
  14.3 3.1 %collective-permute-start.3 = (f32[288,128]{1,0:T(8,128)S(1)}, f32[288,128]{1,0:T(8,128)S(1)}, u32[]{:S(2)}, u32[]{:S(2)}) collective-permute-start(f32[288,128]{1,0:T(8,128)S(1)} %get-tuple-element.9), channel_id=1, source_target_pairs={{0,7},{1,0},{2,1},{3,2},{4,3},{5,4},{6,5},{7,6},{8,15},{9,8},{10,9... | collective-permute-start | bytes 442376 | tf_op jit(solution)/shard_map/ppermute | solution.py:256
  17.4 0.0 copy-done.1
  17.4 0.0 copy-done
  17.4 0.6 turn.1
  18.1 2.6 %collective-permute-done.2.west_ref = f32[288,128]{1,0:T(8,128)S(1)} collective-permute-done((f32[288,128]{1,0:T(8,128)S(1)}, f32[288,128]{1,0:T(8,128)S(1)}, u32[]{:S(2)}, u32[]{:S(2)}) %collective-permute-start.2) | collective-permute-done | bytes 147488 | tf_op jit(solution)/shard_map/ppermute | solution.py:256
  20.6 0.5 collective-permute-done.3.east_ref
  21.1 0.0 copy-done.3
  21.1 0.0 copy-start.4
  21.1 0.0 copy-start.5
  21.1 0.0 copy-start.6
  21.1 30.3 %columns.1 = (f32[1280,128]{1,0:T(8,128)}, f32[32,1024]{1,0:T(8,128)S(1)}) custom-call(f32[1408,128]{1,0:T(8,128)S(1)} %lay.1.main_ref, f32[880,128]{1,0:T(8,128)S(1)} %collective-permute-done.north_ref, f32[880,128]{1,0:T(8,128)S(1)} %collective-permute-done.1.south_ref, f32[288,128]{1,0:T(8,128)S(1)} %collective-permute-done.2.west_ref, ...), custom_call_target="tpu_custom_call" | custom-call | tf_op jit(solution)/shard_map/columns/pallas_call | solution.py:307
  51.4 0.1 copy.11
  51.5 19.0 %all_to_all.11 = f32[32,1,1024]{2,1,0:T(1,128)S(1)} all-to-all(f32[32,1,1024]{2,1,0:T(1,128)S(1)} %copy.11), channel_id=1, replica_groups=mesh['lat'=4,'lon'=8] {'lat','lon'}, dimensions={0} | all-to-all | bytes 262144 | tf_op jit(solution)/shard_map/all_to_all | solution.py:394
  70.6 0.0 copy-done.4
  70.6 0.0 copy-done.5
  70.6 0.0 copy-done.6
  70.6 5.4 %scatter_misfit.1 = f32[64,128]{1,0:T(8,128)} custom-call(f32[32,1024]{1,0:T(8,128)S(1)} %bitcast.15, s32[32,1024]{1,0:T(8,128)S(1)} %copy-done.4, f32[64,128]{1,0:T(8,128)S(1)} %bitcast.18, f32[64,128]{1,0:T(8,128)S(1)} %bitcast.19), custom_call_target="tpu_custom_call" | custom-call | tf_op jit(solution)/shard_map/scatter_misfit/pallas_call | solution.py:368
  (1 shorter events, 0.0 us)
Async XLA Ops:
  0.6 1.1 %copy-start.2 = (f32[20,4,16,128]{3,2,1,0:T(8,128)S(1)}, f32[20,4,16,128]{3,2,1,0:T(8,128)}, u32[]{:S(2)}) copy-start(f32[20,4,16,128]{3,2,1,0:T(8,128)} %param.9) | copy-start | bytes 1966084
  1.7 0.7 copy-start.7
  2.4 0.7 copy-start.8
  3.3 14.1 %copy-start.1 = (f32[8,32,1024]{2,1,0:T(8,128)S(1)}, f32[8,32,1024]{2,1,0:T(8,128)}, u32[]{:S(2)}) copy-start(f32[8,32,1024]{2,1,0:T(8,128)} %param.14) | copy-start | bytes 3145732
  3.4 14.0 %copy-start = (s32[8,32,1024]{2,1,0:T(8,128)S(1)}, s32[8,32,1024]{2,1,0:T(8,128)}, u32[]{:S(2)}) copy-start(s32[8,32,1024]{2,1,0:T(8,128)} %param.13) | copy-start | bytes 3145732
  3.4 4.5 %collective-permute-start.1 = (f32[880,128]{1,0:T(8,128)S(1)}, f32[880,128]{1,0:T(8,128)S(1)}, u32[]{:S(2)}, u32[]{:S(2)}) collective-permute-start(f32[880,128]{1,0:T(8,128)S(1)} %get-tuple-element.14), channel_id=1, source_target_pairs={{8,0},{16,8},{24,16},{9,1},{17,9},{25,17},{10,2},{18,10},{26,18},{... | collective-permute-start | bytes 1351688 | tf_op jit(solution)/shard_map/ppermute | solution.py:256
  4.8 4.5 %collective-permute-start = (f32[880,128]{1,0:T(8,128)S(1)}, f32[880,128]{1,0:T(8,128)S(1)}, u32[]{:S(2)}, u32[]{:S(2)}) collective-permute-start(f32[880,128]{1,0:T(8,128)S(1)} %get-tuple-element.15), channel_id=1, source_target_pairs={{0,8},{8,16},{16,24},{1,9},{9,17},{17,25},{2,10},{10,18},{18,26},{... | collective-permute-start | bytes 1351688 | tf_op jit(solution)/shard_map/ppermute | solution.py:256
  11.3 9.8 %copy-start.3 = (f32[20,16,128]{2,1,0:T(8,128)S(1)}, f32[20,16,128]{2,1,0:T(8,128)}, u32[]{:S(2)}) copy-start(f32[20,16,128]{2,1,0:T(8,128)} %param.12) | copy-start | bytes 491524
  11.3 9.3 %collective-permute-start.2 = (f32[288,128]{1,0:T(8,128)S(1)}, f32[288,128]{1,0:T(8,128)S(1)}, u32[]{:S(2)}, u32[]{:S(2)}) collective-permute-start(f32[288,128]{1,0:T(8,128)S(1)} %get-tuple-element.8), channel_id=1, source_target_pairs={{0,1},{1,2},{2,3},{3,4},{4,5},{5,6},{6,7},{7,0},{8,9},{9,10},{10,1... | collective-permute-start | bytes 442376 | tf_op jit(solution)/shard_map/ppermute | solution.py:256
  14.3 6.7 %collective-permute-start.3 = (f32[288,128]{1,0:T(8,128)S(1)}, f32[288,128]{1,0:T(8,128)S(1)}, u32[]{:S(2)}, u32[]{:S(2)}) collective-permute-start(f32[288,128]{1,0:T(8,128)S(1)} %get-tuple-element.9), channel_id=1, source_target_pairs={{0,7},{1,0},{2,1},{3,2},{4,3},{5,4},{6,5},{7,6},{8,15},{9,8},{10,9... | collective-permute-start | bytes 442376 | tf_op jit(solution)/shard_map/ppermute | solution.py:256
  21.1 49.5 %copy-start.4 = (s32[32,1024]{1,0:T(8,128)S(1)}, s32[32,1024]{1,0:T(8,128)}, u32[]{:S(2)}) copy-start(s32[32,1024]{1,0:T(8,128)} %tgt_ref.1) | copy-start | bytes 393220
  21.1 49.5 %copy-start.5 = (f32[8192]{0:T(1024)S(1)}, f32[8192]{0:T(1024)}, u32[]{:S(2)}) copy-start(f32[8192]{0:T(1024)} %param.16) | copy-start | bytes 98308
  21.1 49.6 %copy-start.6 = (f32[8192]{0:T(1024)S(1)}, f32[8192]{0:T(1024)}, u32[]{:S(2)}) copy-start(f32[8192]{0:T(1024)} %param.17) | copy-start | bytes 98308

commit v4 on v3

--- a/solution.py
+++ b/solution.py
@@ -123,23 +123,31 @@
         if step % 2:
             old, new = new, old
 
-        def one_row(r, carry, old=old, new=new):
-            at = pl.ds(pl.multiple_of(r * SUB, SUB), SUB)
-            c = [coefs[k, at, :] for k in range(10)]
+        def two_rows(turn, carry, old=old, new=new, first=step + 1):
+            r = first + 2 * turn
+            c = [
+                [coefs[k, pl.ds(pl.multiple_of((r + d) * SUB, SUB), SUB), :] for k in range(10)]
+                for d in range(2)
+            ]
             for g in range(groups - 1):
-                mid = pl.ds(pl.multiple_of(r * layers + g * SUB, SUB), SUB)
-                up = pl.ds(pl.multiple_of((r - 1) * layers + g * SUB, SUB), SUB)
-                down = pl.ds(pl.multiple_of((r + 1) * layers + g * SUB, SUB), SUB)
-                a, b = old[0][mid, :], old[1][mid, :]
-                both = sides(a, b)
-                for k, cells in enumerate((a, b)):
-                    p = c[5 * k : 5 * k + 5]
-                    total = p[0] * cells + p[1] * old[k][up, :]
-                    other = p[3] * both[k][0] + p[4] * both[k][1]
-                    new[k][mid, :] = (total + p[2] * old[k][down, :]) + other
+                spots = [
+                    pl.ds(pl.multiple_of((r + d) * layers + g * SUB, SUB), SUB)
+                    for d in range(-1, 3)
+                ]
+                cells = [[old[k][spot, :] for spot in spots] for k in range(2)]
+                results = []
+                for d in range(2):
+                    both = sides(cells[0][d + 1], cells[1][d + 1])
+                    for k in range(2):
+                        p = c[d][5 * k : 5 * k + 5]
+                        total = p[0] * cells[k][d + 1] + p[1] * cells[k][d]
+                        other = p[3] * both[k][0] + p[4] * both[k][1]
+                        results.append((k, spots[d + 1], (total + p[2] * cells[k][d + 2]) + other))
+                for k, spot, value in results:
+                    new[k][spot, :] = value
             return carry
 
-        lax.fori_loop(step + 1, tall - 1 - step, one_row, 0, unroll=2)
+        lax.fori_loop(0, (tall - 2 - 2 * step) // 2, two_rows, 0)
 
 
 def solve_columns(rows, layers, done, vert_ref, inc_ref):
@@ -358,7 +366,7 @@
         acc[...] += spread(rec_ref[pl.ds(p, 1), :], tgt_ref[pl.ds(p, 1), :], high)
         return carry
 
-    lax.fori_loop(0, rec_ref.shape[0], one_source, 0, unroll=4)
+    lax.fori_loop(0, rec_ref.shape[0], one_source, 0, unroll=8)
     total = acc[:high] + acc[high : 2 * high] + acc[2 * high :]
     out_ref[...] = (total - obs_ref[...]) * err_ref[...]
 

time: 76.3 us -> 75.5 us (0.990)
  Pallas kernels: 38.5 us -> 37.6 us
where the time goes in v4:
time: 75.5 us; the launch traced here: 75.2 us
  Pallas kernels  37.6 us (50%)
  blocking collectives  19 us (25%)
  starting transfers between devices  10.6 us (14%)
  waiting for transfers between devices  4.38 us (6%)
  local copies, waits for them, and re-layouts  2.72 us (4%)
  between operations  0.76 us (1%)
    pallas_call x1, Pallas kernels, columns_and_partials(): local_call(functools.partial(column_kernel, rows, layers, owners), (float...  30.1 us
    all_to_all x1, blocking collectives, per_device(): lax.all_to_all(partial_value, ('lat', 'lon'), split_axis=0, concat_axis=0...  19 us
    ppermute x4, starting transfers between devices, shift(): return lax.ppermute(block, axis, pairs)  10.6 us
    pallas_call x1, Pallas kernels, scatter_misfit(): pl.pallas_call(scatter_kernel, out_shape=jax.ShapeDtypeStruct((high, LANE...  4.71 us
    ppermute x4, waiting for transfers between devices, shift(): return lax.ppermute(block, axis, pairs)  4.38 us
    unnamed x19, local copies, waits for them, and re-layouts  2.53 us
    pallas_call x1, Pallas kernels, columns_and_partials(): local_call(functools.partial(pack_kernel, rows, groups), (floats(tall * S...  1.99 us
  transfers between devices with their start and end apart: 4, of which 3 were waited for; matrix products, arithmetic and copies ran while one was open for 0% of the time, Pallas kernels for 1%

profile of v4, /device:TPU:0, one launch (start us, length us, event | category | flops | bytes accessed | tf_op | source)
XLA Modules:
  0.0 75.2 jit_solution(1704971709280305313)
XLA Ops:
  0.6 0.0 copy-start.2
  0.6 1.1 %copy-done.2 = f32[20,4,16,128]{3,2,1,0:T(8,128)S(1)} copy-done((f32[20,4,16,128]{3,2,1,0:T(8,128)S(1)}, f32[20,4,16,128]{3,2,1,0:T(8,128)}, u32[]{:S(2)}) %copy-start.2) | copy-done | bytes 655384
  1.7 0.0 copy-start.7
  1.7 0.7 copy-done.7
  2.4 0.0 copy-start.8
  2.4 0.7 copy-done.8
  3.1 0.2 lay.1.main_ref
  3.3 0.0 copy-start.1
  3.3 0.1 fusion
  3.4 0.0 copy-start
  3.4 1.4 %collective-permute-start.1 = (f32[880,128]{1,0:T(8,128)S(1)}, f32[880,128]{1,0:T(8,128)S(1)}, u32[]{:S(2)}, u32[]{:S(2)}) collective-permute-start(f32[880,128]{1,0:T(8,128)S(1)} %get-tuple-element.14), channel_id=1, source_target_pairs={{8,0},{16,8},{24,16},{9,1},{17,9},{25,17},{10,2},{18,10},{26,18},{... | collective-permute-start | bytes 1351688 | tf_op jit(solution)/shard_map/ppermute | solution.py:264
  4.8 3.1 %collective-permute-start = (f32[880,128]{1,0:T(8,128)S(1)}, f32[880,128]{1,0:T(8,128)S(1)}, u32[]{:S(2)}, u32[]{:S(2)}) collective-permute-start(f32[880,128]{1,0:T(8,128)S(1)} %get-tuple-element.15), channel_id=1, source_target_pairs={{0,8},{8,16},{16,24},{1,9},{9,17},{17,25},{2,10},{10,18},{18,26},{... | collective-permute-start | bytes 1351688 | tf_op jit(solution)/shard_map/ppermute | solution.py:264
  7.9 0.0 collective-permute-done.1.south_ref
  7.9 1.4 %collective-permute-done.north_ref = f32[880,128]{1,0:T(8,128)S(1)} collective-permute-done((f32[880,128]{1,0:T(8,128)S(1)}, f32[880,128]{1,0:T(8,128)S(1)}, u32[]{:S(2)}, u32[]{:S(2)}) %collective-permute-start) | collective-permute-done | bytes 450592 | tf_op jit(solution)/shard_map/ppermute | solution.py:264
  9.3 2.0 %pack.1 = (f32[288,128]{1,0:T(8,128)S(1)}, f32[288,128]{1,0:T(8,128)S(1)}) custom-call(f32[1408,128]{1,0:T(8,128)S(1)} %lay.1.main_ref, f32[880,128]{1,0:T(8,128)S(1)} %collective-permute-done.north_ref, f32[880,128]{1,0:T(8,128)S(1)} %collective-permute-done.1.south_ref), custom_call_target="tpu_custom_call" | custom-call | tf_op jit(solution)/shard_map/pack/pallas_call | solution.py:298
  11.3 0.0 copy-start.3
  11.3 3.0 %collective-permute-start.2 = (f32[288,128]{1,0:T(8,128)S(1)}, f32[288,128]{1,0:T(8,128)S(1)}, u32[]{:S(2)}, u32[]{:S(2)}) collective-permute-start(f32[288,128]{1,0:T(8,128)S(1)} %get-tuple-element.8), channel_id=1, source_target_pairs={{0,1},{1,2},{2,3},{3,4},{4,5},{5,6},{6,7},{7,0},{8,9},{9,10},{10,1... | collective-permute-start | bytes 442376 | tf_op jit(solution)/shard_map/ppermute | solution.py:264
  14.3 3.1 %collective-permute-start.3 = (f32[288,128]{1,0:T(8,128)S(1)}, f32[288,128]{1,0:T(8,128)S(1)}, u32[]{:S(2)}, u32[]{:S(2)}) collective-permute-start(f32[288,128]{1,0:T(8,128)S(1)} %get-tuple-element.9), channel_id=1, source_target_pairs={{0,7},{1,0},{2,1},{3,2},{4,3},{5,4},{6,5},{7,6},{8,15},{9,8},{10,9... | collective-permute-start | bytes 442376 | tf_op jit(solution)/shard_map/ppermute | solution.py:264
  17.4 0.0 copy-done.1
  17.4 0.0 copy-done
  17.4 0.6 turn.1
  18.1 2.6 %collective-permute-done.2.west_ref = f32[288,128]{1,0:T(8,128)S(1)} collective-permute-done((f32[288,128]{1,0:T(8,128)S(1)}, f32[288,128]{1,0:T(8,128)S(1)}, u32[]{:S(2)}, u32[]{:S(2)}) %collective-permute-start.2) | collective-permute-done | bytes 147488 | tf_op jit(solution)/shard_map/ppermute | solution.py:264
  20.6 0.5 collective-permute-done.3.east_ref
  21.1 0.0 copy-done.3
  21.1 0.0 copy-start.4
  21.1 0.0 copy-start.5
  21.1 0.0 copy-start.6
  21.1 30.1 %columns.1 = (f32[1280,128]{1,0:T(8,128)}, f32[32,1024]{1,0:T(8,128)S(1)}) custom-call(f32[1408,128]{1,0:T(8,128)S(1)} %lay.1.main_ref, f32[880,128]{1,0:T(8,128)S(1)} %collective-permute-done.north_ref, f32[880,128]{1,0:T(8,128)S(1)} %collective-permute-done.1.south_ref, f32[288,128]{1,0:T(8,128)S(1)} %collective-permute-done.2.west_ref, ...), custom_call_target="tpu_custom_call" | custom-call | tf_op jit(solution)/shard_map/columns/pallas_call | solution.py:315
  51.2 0.1 copy.11
  51.3 19.0 %all_to_all.11 = f32[32,1,1024]{2,1,0:T(1,128)S(1)} all-to-all(f32[32,1,1024]{2,1,0:T(1,128)S(1)} %copy.11), channel_id=1, replica_groups=mesh['lat'=4,'lon'=8] {'lat','lon'}, dimensions={0} | all-to-all | bytes 262144 | tf_op jit(solution)/shard_map/all_to_all | solution.py:402
  70.4 0.0 copy-done.4
  70.4 0.0 copy-done.5
  70.4 0.0 copy-done.6
  70.4 4.7 %scatter_misfit.1 = f32[64,128]{1,0:T(8,128)} custom-call(f32[32,1024]{1,0:T(8,128)S(1)} %bitcast.15, s32[32,1024]{1,0:T(8,128)S(1)} %copy-done.4, f32[64,128]{1,0:T(8,128)S(1)} %bitcast.18, f32[64,128]{1,0:T(8,128)S(1)} %bitcast.19), custom_call_target="tpu_custom_call" | custom-call | tf_op jit(solution)/shard_map/scatter_misfit/pallas_call | solution.py:376
  (1 shorter events, 0.0 us)
Async XLA Ops:
  0.6 1.1 %copy-start.2 = (f32[20,4,16,128]{3,2,1,0:T(8,128)S(1)}, f32[20,4,16,128]{3,2,1,0:T(8,128)}, u32[]{:S(2)}) copy-start(f32[20,4,16,128]{3,2,1,0:T(8,128)} %param.9) | copy-start | bytes 1966084
  1.7 0.7 copy-start.7
  2.4 0.7 copy-start.8
  3.3 14.1 %copy-start.1 = (f32[8,32,1024]{2,1,0:T(8,128)S(1)}, f32[8,32,1024]{2,1,0:T(8,128)}, u32[]{:S(2)}) copy-start(f32[8,32,1024]{2,1,0:T(8,128)} %param.14) | copy-start | bytes 3145732
  3.4 14.0 %copy-start = (s32[8,32,1024]{2,1,0:T(8,128)S(1)}, s32[8,32,1024]{2,1,0:T(8,128)}, u32[]{:S(2)}) copy-start(s32[8,32,1024]{2,1,0:T(8,128)} %param.13) | copy-start | bytes 3145732
  3.4 4.5 %collective-permute-start.1 = (f32[880,128]{1,0:T(8,128)S(1)}, f32[880,128]{1,0:T(8,128)S(1)}, u32[]{:S(2)}, u32[]{:S(2)}) collective-permute-start(f32[880,128]{1,0:T(8,128)S(1)} %get-tuple-element.14), channel_id=1, source_target_pairs={{8,0},{16,8},{24,16},{9,1},{17,9},{25,17},{10,2},{18,10},{26,18},{... | collective-permute-start | bytes 1351688 | tf_op jit(solution)/shard_map/ppermute | solution.py:264
  4.8 4.5 %collective-permute-start = (f32[880,128]{1,0:T(8,128)S(1)}, f32[880,128]{1,0:T(8,128)S(1)}, u32[]{:S(2)}, u32[]{:S(2)}) collective-permute-start(f32[880,128]{1,0:T(8,128)S(1)} %get-tuple-element.15), channel_id=1, source_target_pairs={{0,8},{8,16},{16,24},{1,9},{9,17},{17,25},{2,10},{10,18},{18,26},{... | collective-permute-start | bytes 1351688 | tf_op jit(solution)/shard_map/ppermute | solution.py:264
  11.3 9.8 %copy-start.3 = (f32[20,16,128]{2,1,0:T(8,128)S(1)}, f32[20,16,128]{2,1,0:T(8,128)}, u32[]{:S(2)}) copy-start(f32[20,16,128]{2,1,0:T(8,128)} %param.12) | copy-start | bytes 491524
  11.3 9.3 %collective-permute-start.2 = (f32[288,128]{1,0:T(8,128)S(1)}, f32[288,128]{1,0:T(8,128)S(1)}, u32[]{:S(2)}, u32[]{:S(2)}) collective-permute-start(f32[288,128]{1,0:T(8,128)S(1)} %get-tuple-element.8), channel_id=1, source_target_pairs={{0,1},{1,2},{2,3},{3,4},{4,5},{5,6},{6,7},{7,0},{8,9},{9,10},{10,1... | collective-permute-start | bytes 442376 | tf_op jit(solution)/shard_map/ppermute | solution.py:264
  14.3 6.7 %collective-permute-start.3 = (f32[288,128]{1,0:T(8,128)S(1)}, f32[288,128]{1,0:T(8,128)S(1)}, u32[]{:S(2)}, u32[]{:S(2)}) collective-permute-start(f32[288,128]{1,0:T(8,128)S(1)} %get-tuple-element.9), channel_id=1, source_target_pairs={{0,7},{1,0},{2,1},{3,2},{4,3},{5,4},{6,5},{7,6},{8,15},{9,8},{10,9... | collective-permute-start | bytes 442376 | tf_op jit(solution)/shard_map/ppermute | solution.py:264
  21.1 49.4 %copy-start.4 = (s32[32,1024]{1,0:T(8,128)S(1)}, s32[32,1024]{1,0:T(8,128)}, u32[]{:S(2)}) copy-start(s32[32,1024]{1,0:T(8,128)} %tgt_ref.1) | copy-start | bytes 393220
  21.1 49.4 %copy-start.5 = (f32[8192]{0:T(1024)S(1)}, f32[8192]{0:T(1024)}, u32[]{:S(2)}) copy-start(f32[8192]{0:T(1024)} %param.16) | copy-start | bytes 98308
  21.1 49.4 %copy-start.6 = (f32[8192]{0:T(1024)S(1)}, f32[8192]{0:T(1024)}, u32[]{:S(2)}) copy-start(f32[8192]{0:T(1024)} %param.17) | copy-start | bytes 98308
